TPU v7x, 128 devices: a whole 4x4x4 slice. The times are simulated.
128 devices in a mesh: nest: 4 (over z_lo, core), tile: 32 (over z_hi, x, y).
Axes of the slice: x: 4, y: 4, z: 4 (z_hi: 2, z_lo: 2; z = z_hi * 2 + z_lo), core: 2. Of those that a mesh axis runs over, the one named last changes fastest.
Arguments:
- nest_state: bfloat16 [4, 384, 512, 512], P('nest', None, 'tile'), may hold values from -6 to 6
- parent_state: bfloat16 [384, 16384], P(None, ('nest', 'tile')), may hold values from -6 to 6
- mix_weight: bfloat16 [384, 384], replicated, may hold values from -0.3125 to 0.3125
- intersection: int32 [4, 32, 4], P('nest', 'tile'), may hold values from 0 to 11
- interp_weight: bfloat16 [4, 32, 4, 128, 512], P('nest', 'tile'), may hold values from -0.25 to 0.25
- avg_weight: bfloat16 [4, 32, 4, 512, 128], P('nest', 'tile'), may hold values from -0.25 to 0.25
- land_mask: int32 [4, 512, 512], P('nest', 'tile'), may hold values 0 or 1
Outputs:
- nest_out: bfloat16 [4, 384, 512, 512], P('nest', None, 'tile')
- parent_out: bfloat16 [384, 16384], P(None, ('nest', 'tile'))
All inputs are finite; a program needn't handle non-finite values. No bound on the sum of `land_mask` on one device may be relied on, other than what follows from the above.
Results may differ from a plain program's by a relative error of at most 0.012.
Values may be sent and summed in bfloat16 or wider, within the bound.
A program may use at most 192 MiB of HBM per device.

v0:
```python
import jax
import jax.numpy as jnp
from jax import lax
from jax.sharding import PartitionSpec as P

BW = 16
NSUB = 2


def passed_along(value, axis, steps):
    count = lax.axis_size(axis)
    pairs = [(source, (source + steps) % count) for source in range(count)]
    return lax.ppermute(value, axis, pairs)


def with_halo(value, sides, width, wrap):
    for axis, dim in sides:
        peers, length = (lax.axis_size(axis), value.shape[dim])
        up = [(i, (i + 1) % peers) for i in range(peers if wrap else peers - 1)]
        down = [(j, i) for i, j in up]
        last = lax.slice_in_dim(value, length - width, length, axis=dim)
        initial = lax.slice_in_dim(value, 0, width, axis=dim)
        before = lax.ppermute(last, axis, up)
        after = lax.ppermute(initial, axis, down)
        value = jnp.concatenate([before, value, after], axis=dim)
    return value


def laplace(padded):
    center = padded[:, 1:-1]
    cols = jnp.pad(center, ((0, 0), (0, 0), (1, 1)))
    along_rows = padded[:, 2:] + padded[:, :-2] - 2.0 * center
    along_cols = cols[:, :, 2:] + cols[:, :, :-2] - 2.0 * center
    return 0.4 * along_rows + 0.05 * along_cols


def advance(state, padded, factor, strip, mixing):
    channels = state.shape[0]
    width = state.shape[2]
    rounded = state.astype(jnp.bfloat16)
    mixed = jnp.dot(
        mixing, rounded.reshape(channels, -1), preferred_element_type=jnp.float32
    ).reshape(state.shape)
    moved = state + factor[None] * (0.5 * mixed + laplace(padded))
    zone = strip.shape[2] // 2
    column = jnp.arange(width, dtype=jnp.int32)
    west_ramp = (zone - column.astype(jnp.float32)) / zone
    east_ramp = (zone - (width - 1 - column).astype(jnp.float32)) / zone
    ramp_full = jnp.where(
        column < zone, west_ramp, jnp.where(column >= width - zone, east_ramp, 0.0)
    )
    strip_wide = strip.astype(jnp.float32)
    middle = jnp.zeros((channels, state.shape[1], width - 2 * zone), jnp.float32)
    strip_full = jnp.concatenate([strip_wide[:, :, :zone], middle, strip_wide[:, :, zone:]], axis=2)
    return moved + ramp_full * (strip_full - moved)


def side_move(terms, by):
    return passed_along(terms.astype(jnp.bfloat16), "tile", by).astype(terms.dtype)


def shards(
    nest_state, parent_state, mix_weight, intersection, interp_weight, avg_weight, land_mask
):
    channels = mix_weight.shape[0]
    rows = nest_state.shape[2]
    width = nest_state.shape[3]
    tile_cells = parent_state.shape[1]
    groups = lax.axis_size("nest")
    slots = intersection.shape[2]
    own = parent_state[None]
    grouped = lax.all_gather(own, "nest", axis=0, tiled=True)
    candidates = with_halo(grouped, (("tile", 2),), tile_cells, True)
    candidates = candidates.reshape(groups, channels, 3, tile_cells)
    picks = intersection[0, 0]
    selector = picks[:, None] == jnp.arange(3 * groups, dtype=jnp.int32)[None, :]
    onehot_low = selector.astype(jnp.bfloat16).reshape(slots, groups, 3)
    picked = jnp.einsum(
        "kgo,gmop->kmp", onehot_low, candidates, preferred_element_type=jnp.float32
    ).astype(jnp.bfloat16)
    strip = jnp.einsum(
        "kmp,kps->ms", picked, interp_weight[0, 0], preferred_element_type=jnp.float32
    )
    strip = strip.astype(jnp.bfloat16).reshape(channels, rows, 2 * BW)
    state = nest_state[0].astype(jnp.float32)
    factor = jnp.where(land_mask[0] == 1, 0.5, 1.0).astype(jnp.float32)
    for step in range(NSUB):
        padded = with_halo(state.astype(jnp.bfloat16), (("tile", 1),), 1, False).astype(state.dtype)
        state = advance(state, padded, factor, strip, mix_weight)
    nest_out = state.astype(jnp.bfloat16)[None]
    row_sums = state.reshape(channels, rows // 4, 4, width).sum(axis=2)
    pooling = (
        jnp.arange(width, dtype=jnp.int32)[:, None] // 4
        == jnp.arange(width // 4, dtype=jnp.int32)[None, :]
    ).astype(jnp.float32)
    block_sums = jnp.dot(row_sums.reshape(-1, width), pooling, precision=lax.Precision.HIGHEST)
    coarse = (block_sums / 16.0).astype(jnp.bfloat16).reshape(channels, -1)
    feed = jnp.einsum("mq,kqp->kmp", coarse, avg_weight[0, 0], preferred_element_type=jnp.float32)
    onehot_full = selector.astype(jnp.float32)
    spread = jnp.einsum("kc,kmp->cmp", onehot_full, feed, precision=lax.Precision.HIGHEST)
    spread = spread.reshape(groups, 3, channels, tile_cells)
    combined = spread[:, 1] + side_move(spread[:, 0], -1) + side_move(spread[:, 2], 1)
    totals = lax.psum_scatter(
        combined.astype(jnp.bfloat16), "nest", scatter_dimension=0, tiled=True
    ).astype(jnp.float32)[0]
    parent_out = (parent_state.astype(jnp.float32) + totals).astype(jnp.bfloat16)
    return (nest_out, parent_out)


def solution(mesh):
    in_specs = (
        P("nest", None, "tile", None),
        P(None, ("nest", "tile")),
        P(),
        P("nest", "tile", None),
        P("nest", "tile", None, None, None),
        P("nest", "tile", None, None, None),
        P("nest", "tile", None),
    )
    out_specs = (P("nest", None, "tile", None), P(None, ("nest", "tile")))
    return jax.shard_map(shards, mesh=mesh, in_specs=in_specs, out_specs=out_specs, check_vma=False)
```

profile of v0, /device:TPU:1, one launch (start us, length us, event | category | flops | bytes accessed | tf_op | source)
XLA Modules:
  0.0 293.3 jit_solution(13835398207075610362)
XLA Ops:
  7.2 0.0 reduce-scatter.2.cloned.1.call-start
  7.2 8.6 %all-gather = bf16[1536,128]{1,0:T(8,128)(2,1)S(1)} all-gather(bf16[384,128]{1,0:T(8,128)(2,1)} %param.8), channel_id=2, replica_groups=mesh['nest'=4,'tile'=32] {'nest'}, dimensions={0}, use_global_device_ids=true | all-gather | bytes 491520 | tf_op jit(solution)/shard_map/all_gather | solution.py:72
  15.8 7.9 %collective-permute-start.3 = (bf16[4,384,128]{2,1,0:T(8,128)(2,1)S(1)}, bf16[4,384,128]{2,1,0:T(8,128)(2,1)S(1)}, u32[]{:S(2)}, u32[]{:S(2)}) collective-permute-start(bf16[4,384,128]{2,1,0:T(8,128)(2,1)S(1)} %bitcast.96), channel_id=1, source_target_pairs={{1,0},{2,1},{3,2},{4,3},{5,4},{6,5},{7,6},{8,7},{9,8},{10,9},{11,1... | collective-permute-start | bytes 1179656 | tf_op jit(solution)/shard_map/ppermute | solution.py:24
  23.8 6.3 %copy.84 = bf16[1,384,16,512]{3,1,2,0:T(8,128)(2,1)S(1)} copy(bf16[1,384,16,512]{3,2,1,0:T(8,128)(2,1)} %param.7) | data formatting | bytes 12582912 | tf_op args[0]
  30.1 2.7 copy-done.2
  32.8 0.9 fusion.58
  33.7 1.3 collective-permute-start.1
  35.0 5.0 %collective-permute-start = (bf16[384,1,512]{2,0,1:T(8,128)(2,1)}, bf16[384,1,512]{2,0,1:T(8,128)(2,1)}, u32[]{:S(2)}, u32[]{:S(2)}) collective-permute-start(bf16[384,1,512]{2,0,1:T(8,128)(2,1)} %get-tuple-element.16), channel_id=1, source_target_pairs={{0,1},{1,2},{2,3},{3,4},{4,5},{5,6},{6,7},{7,8},{8,9},{9,10},{10,1... | collective-permute-start | bytes 1179656 | tf_op jit(solution)/shard_map/ppermute | solution.py:23
  40.1 10.0 %copy.76 = bf16[48,8,16,512]{3,1,2,0:T(8,128)(2,1)} copy(bf16[48,8,16,512]{3,2,1,0:T(8,128)(2,1)S(1)} %bitcast.88) | data formatting | bytes 12582912
  50.1 9.2 %copy.56 = bf16[8192,384]{1,0:T(8,128)(2,1)} copy(bf16[8192,384]{0,1:T(8,128)(2,1)} %bitcast.90) | data formatting | bytes 12582912 | tf_op jit(solution)/shard_map/dot_general | solution.py:41
  59.2 0.1 pad.13.clone
  59.3 1.2 pad_maximum_fusion.1
  60.5 0.8 copy.57
  61.3 0.9 copy.58
  62.2 1.0 fusion.27
  63.2 0.4 fusion.26
  63.6 0.3 copy.60
  63.9 0.1 fusion.59
  64.0 2.2 copy.73
  66.2 2.3 copy.72
  68.4 9.1 %maximum_convert_fusion = f32[384,18,512]{2,0,1:T(8,128)} fusion(bf16[384,1,512]{2,0,1:T(8,128)(2,1)} %collective-permute-done.1, bf16[384,16,512]{2,0,1:T(8,128)(2,1)} %bitcast.85, bf16[384,1,512]{2,0,1:T(8,128)(2,1)} %collective-permute-done), kind=kLoop, calls=%fused_computation.33 | loop fusion | flops 10616832 | bytes 21233664 | tf_op jit(solution)/shard_map/convert_element_type | solution.py:88
  77.6 11.2 %slice.84 = f32[384,16,512]{2,0,1:T(8,128)} slice(f32[384,18,512]{2,0,1:T(8,128)} %maximum_convert_fusion), slice={[0:384], [1:17], [0:512]} | slice | bytes 25165824 | tf_op jit(solution)/shard_map/slice | solution.py:30
  88.8 34.8 %fusion.60 = (bf16[384,16,512]{2,0,1:T(8,128)(2,1)}, f32[384,16,512]{2,0,1:T(8,128)}) fusion(f32[384,16,16]{2,0,1:T(8,128)} %copy.73, f32[512]{0:T(512)S(1)} %pad.13.clone, f32[384,16,16]{2,0,1:T(8,128)} %copy.72, f32[512]{0:T(512)S(1)} %fusion.47, f32[384,16,512]{2,0,1:T(8,128)} %slice.84, f32[384,18,512]{2,0,1:T(8,128)} %maximum_convert_fusion, ...), kind=kOutput, calls=%fused_computation.92 | convolution fusion | flops 2475687936 | bytes 70324224 | tf_op jit(solution)/shard_map/dot_general | solution.py:41
  123.6 8.6 %copy.63 = bf16[384,16,512]{0,2,1:T(8,128)(2,1)} copy(bf16[384,16,512]{2,0,1:T(8,128)(2,1)} %get-tuple-element.22) | data formatting | bytes 12582912 | tf_op jit(solution)/shard_map/convert_element_type | solution.py:40
  132.2 1.2 fusion.57
  133.4 1.3 collective-permute-start.5
  134.7 4.2 %collective-permute-start.4 = (bf16[384,1,512]{2,0,1:T(8,128)(2,1)S(1)}, bf16[384,1,512]{2,0,1:T(8,128)(2,1)S(1)}, u32[]{:S(2)}, u32[]{:S(2)}) collective-permute-start(bf16[384,1,512]{2,0,1:T(8,128)(2,1)S(1)} %get-tuple-element.14), channel_id=1, source_target_pairs={{0,1},{1,2},{2,3},{3,4},{4,5},{5,6},{6,7},{7,8},{8,9},{9,10},{10,1... | collective-permute-start | bytes 1179656 | tf_op jit(solution)/shard_map/ppermute | solution.py:23
  138.9 11.3 %convolution_multiply_fusion = f32[8192,384]{1,0:T(8,128)} fusion(bf16[384,8192]{0,1:T(8,128)(2,1)} %bitcast.83, bf16[384,384]{1,0:T(8,128)(2,1)S(1)} %copy-done.5), kind=kOutput, calls=%fused_computation.32 | convolution fusion | flops 2419064832 | bytes 19169280 | tf_op jit(solution)/shard_map/dot_general | solution.py:41
  150.2 12.6 %copy.64 = f32[384,16,512]{2,0,1:T(8,128)} copy(f32[384,16,512]{0,2,1:T(8,128)} %bitcast.82) | data formatting | bytes 25165824 | tf_op jit(solution)/shard_map/mul | solution.py:44
  162.7 9.0 %maximum_convert_fusion.1 = f32[384,18,512]{2,0,1:T(8,128)} fusion(bf16[384,1,512]{2,0,1:T(8,128)(2,1)S(1)} %collective-permute-done.5, bf16[384,16,512]{2,0,1:T(8,128)(2,1)} %get-tuple-element.22, bf16[384,1,512]{2,0,1:T(8,128)(2,1)S(1)} %collective-permute-done.4), kind=kLoop, calls=%fused_computation.34 | loop fusion | flops 10616832 | bytes 21233664 | tf_op jit(solution)/shard_map/convert_element_type | solution.py:88
  171.7 11.2 %slice.91 = f32[384,16,512]{2,0,1:T(8,128)} slice(f32[384,18,512]{2,0,1:T(8,128)} %maximum_convert_fusion.1), slice={[0:384], [1:17], [0:512]} | slice | bytes 25165824 | tf_op jit(solution)/shard_map/slice | solution.py:30
  182.9 38.8 %bitcast_reduce_fusion = (f32[384,4,512]{2,0,1:T(8,128)}, bf16[384,16,512]{2,0,1:T(8,128)(2,1)}) fusion(f32[384,16,16]{2,0,1:T(8,128)} %copy.73, f32[512]{0:T(512)S(1)} %pad.13.clone, f32[384,16,16]{2,0,1:T(8,128)} %copy.72, f32[512]{0:T(512)S(1)} %fusion.47, f32[384,16,512]{2,0,1:T(8,128)} %get-tuple-element.23, f32[384,16,512]{2,0,1:T(8,128)} %copy.64, ...), kind=kLoop, calls=%fused_computation.31 | loop fusion | flops 55836672 | bytes 73175040 | tf_op jit(solution)/shard_map/reduce_sum | solution.py:91
  221.7 5.6 %copy.65 = f32[384,4,512]{2,1,0:T(4,128)} copy(f32[384,4,512]{2,0,1:T(8,128)} %get-tuple-element.12) | data formatting | bytes 6291456 | tf_op jit(solution)/shard_map/reduce_sum | solution.py:91
  227.3 5.1 %reshape.113 = f32[1536,512]{1,0:T(8,128)} reshape(f32[384,4,512]{2,1,0:T(4,128)} %copy.65) | data formatting | bytes 6291456 | tf_op jit(solution)/shard_map/reshape | solution.py:96
  232.4 3.5 %fusion.24 = bf16[1536,128]{1,0:T(8,128)(2,1)S(1)} fusion(f32[1536,512]{1,0:T(8,128)} %reshape.113, s32[512]{0:T(512)S(1)} %add_select_fusion), kind=kOutput, calls=%fused_computation.38 | convolution fusion | flops 1208418304 | bytes 3540992 | tf_op jit(solution)/shard_map/dot_general | solution.py:96
  235.9 0.2 reshape.123
  236.2 0.4 convolution_bitcast_fusion
  236.6 2.0 fusion.31
  238.6 0.8 copy.67
  239.3 0.2 convert.6
  239.5 0.1 slice_bitcast_fusion.2
  239.6 0.1 collective-permute-start.7
  239.7 7.2 %collective-permute-start.6 = (bf16[4,384,128]{2,1,0:T(8,128)(2,1)S(1)}, bf16[4,384,128]{2,1,0:T(8,128)(2,1)S(1)}, u32[]{:S(2)}, u32[]{:S(2)}) collective-permute-start(bf16[4,384,128]{2,1,0:T(8,128)(2,1)S(1)} %get-tuple-element.18), channel_id=1, source_target_pairs={{0,31},{1,0},{2,1},{3,2},{4,3},{5,4},{6,5},{7,6},{8,7},{9,8},{10,9... | collective-permute-start | bytes 1179656 | tf_op jit(solution)/shard_map/ppermute | solution.py:13
  246.9 7.6 %collective-permute-done.7 = bf16[4,384,128]{2,1,0:T(8,128)(2,1)S(1)} collective-permute-done((bf16[4,384,128]{2,1,0:T(8,128)(2,1)S(1)}, bf16[4,384,128]{2,1,0:T(8,128)(2,1)S(1)}, u32[]{:S(2)}, u32[]{:S(2)}) %collective-permute-start.7) | collective-permute-done | bytes 393248 | tf_op jit(solution)/shard_map/ppermute | solution.py:13
  254.4 0.9 fusion.30
  255.4 9.0 %copy.70 = bf16[1,384,16,512]{3,2,1,0:T(8,128)(2,1)} copy(bf16[1,384,16,512]{3,1,2,0:T(8,128)(2,1)} %bitcast.89) | data formatting | bytes 12582912
  264.4 20.3 %reduce-scatter.2.cloned.1.call-done = bf16[1,384,128]{2,1,0:T(8,128)(2,1)} async-done(((bf16[4,384,128]{2,1,0:T(8,128)(2,1)}), bf16[1,384,128]{2,1,0:T(8,128)(2,1)}) %reduce-scatter.2.cloned.1.call-update) | async-done | bytes 98320 | tf_op jit(solution)/shard_map/reduce_scatter | solution.py:103
  284.6 1.6 fusion.37
  (34 shorter events, 0.1 us)
Async XLA Ops:
  7.2 56.1 %copy-start = (bf16[1,1,4,128,512]{4,3,2,1,0:T(8,128)(2,1)S(1)}, bf16[1,1,4,128,512]{4,3,2,1,0:T(8,128)(2,1)}, u32[]{:S(2)}) copy-start(bf16[1,1,4,128,512]{4,3,2,1,0:T(8,128)(2,1)} %param.11) | copy-start | bytes 1572868
  7.2 32.9 %slice-start = ((s8[6291456]{0:T(1024)(128)(4,1)}), s8[2097152]{0:T(1024)(128)(4,1)S(1)}, s32[]{:S(2)}) async-start(s8[6291456]{0:T(1024)(128)(4,1)} %bitcast.86), calls=%async_computation.2 | async-start | bytes 4194304
  7.2 277.4 %reduce-scatter.2.cloned.1.call-start = ((), (), s32[]{:S(2)}) async-start(), calls=%async_computation.1 | async-start | bytes 491520 | tf_op jit(solution)/shard_map/reduce_scatter | solution.py:103
  15.8 24.3 %slice-start.1 = ((s8[6291456]{0:T(1024)(128)(4,1)}), s8[4194304]{0:T(1024)(128)(4,1)S(1)}, s32[]{:S(2)}) async-start(s8[6291456]{0:T(1024)(128)(4,1)} %bitcast.86), calls=%async_computation.3 | async-start | bytes 8388608
  15.8 43.5 %collective-permute-start.3 = (bf16[4,384,128]{2,1,0:T(8,128)(2,1)S(1)}, bf16[4,384,128]{2,1,0:T(8,128)(2,1)S(1)}, u32[]{:S(2)}, u32[]{:S(2)}) collective-permute-start(bf16[4,384,128]{2,1,0:T(8,128)(2,1)S(1)} %bitcast.96), channel_id=1, source_target_pairs={{1,0},{2,1},{3,2},{4,3},{5,4},{6,5},{7,6},{8,7},{9,8},{10,9},{11,1... | collective-permute-start | bytes 1179656 | tf_op jit(solution)/shard_map/ppermute | solution.py:24
  23.8 35.6 %collective-permute-start.2 = (bf16[4,384,128]{2,1,0:T(8,128)(2,1)S(1)}, bf16[4,384,128]{2,1,0:T(8,128)(2,1)}, u32[]{:S(2)}, u32[]{:S(2)}) collective-permute-start(bf16[4,384,128]{2,1,0:T(8,128)(2,1)S(1)} %bitcast.97), channel_id=1, source_target_pairs={{0,1},{1,2},{2,3},{3,4},{4,5},{5,6},{6,7},{7,8},{8,9},{9,10},{10,1... | collective-permute-start | bytes 1179656 | tf_op jit(solution)/shard_map/ppermute | solution.py:23
  30.1 2.7 copy-start.2
  33.7 34.7 %collective-permute-start.1 = (bf16[384,1,512]{2,0,1:T(8,128)(2,1)}, bf16[384,1,512]{2,0,1:T(8,128)(2,1)}, u32[]{:S(2)}, u32[]{:S(2)}) collective-permute-start(bf16[384,1,512]{2,0,1:T(8,128)(2,1)} %get-tuple-element.17), channel_id=1, source_target_pairs={{1,0},{2,1},{3,2},{4,3},{5,4},{6,5},{7,6},{8,7},{9,8},{10,9},{11,1... | collective-permute-start | bytes 1179656 | tf_op jit(solution)/shard_map/ppermute | solution.py:24
  35.0 33.4 %collective-permute-start = (bf16[384,1,512]{2,0,1:T(8,128)(2,1)}, bf16[384,1,512]{2,0,1:T(8,128)(2,1)}, u32[]{:S(2)}, u32[]{:S(2)}) collective-permute-start(bf16[384,1,512]{2,0,1:T(8,128)(2,1)} %get-tuple-element.16), channel_id=1, source_target_pairs={{0,1},{1,2},{2,3},{3,4},{4,5},{5,6},{6,7},{7,8},{8,9},{9,10},{10,1... | collective-permute-start | bytes 1179656 | tf_op jit(solution)/shard_map/ppermute | solution.py:23
  40.1 19.2 %copy-start.6 = (s32[1,16,512]{2,1,0:T(8,128)S(1)}, s32[1,16,512]{2,1,0:T(8,128)}, u32[]{:S(2)}) copy-start(s32[1,16,512]{2,1,0:T(8,128)} %param.13) | copy-start | bytes 98308
  50.1 12.2 %copy-start.7 = (s32[1,1,4]{2,1,0:T(1,128)S(1)}, s32[1,1,4]{2,1,0:T(1,128)}, u32[]{:S(2)}) copy-start(s32[1,1,4]{2,1,0:T(1,128)} %param.10) | copy-start | bytes 52
  77.6 11.3 %copy-start.5 = (bf16[384,384]{1,0:T(8,128)(2,1)S(1)}, bf16[384,384]{1,0:T(8,128)(2,1)}, u32[]{:S(2)}) copy-start(bf16[384,384]{1,0:T(8,128)(2,1)} %param.9) | copy-start | bytes 884740
  133.4 29.4 %collective-permute-start.5 = (bf16[384,1,512]{2,0,1:T(8,128)(2,1)S(1)}, bf16[384,1,512]{2,0,1:T(8,128)(2,1)S(1)}, u32[]{:S(2)}, u32[]{:S(2)}) collective-permute-start(bf16[384,1,512]{2,0,1:T(8,128)(2,1)S(1)} %get-tuple-element.15), channel_id=1, source_target_pairs={{1,0},{2,1},{3,2},{4,3},{5,4},{6,5},{7,6},{8,7},{9,8},{10,9},{11,1... | collective-permute-start | bytes 1179656 | tf_op jit(solution)/shard_map/ppermute | solution.py:24
  134.7 28.1 %collective-permute-start.4 = (bf16[384,1,512]{2,0,1:T(8,128)(2,1)S(1)}, bf16[384,1,512]{2,0,1:T(8,128)(2,1)S(1)}, u32[]{:S(2)}, u32[]{:S(2)}) collective-permute-start(bf16[384,1,512]{2,0,1:T(8,128)(2,1)S(1)} %get-tuple-element.14), channel_id=1, source_target_pairs={{0,1},{1,2},{2,3},{3,4},{4,5},{5,6},{6,7},{7,8},{8,9},{9,10},{10,1... | collective-permute-start | bytes 1179656 | tf_op jit(solution)/shard_map/ppermute | solution.py:23
  221.7 14.5 %copy-start.3 = (bf16[1,1,4,512,128]{4,3,2,1,0:T(8,128)(2,1)S(1)}, bf16[1,1,4,512,128]{4,3,2,1,0:T(8,128)(2,1)}, u32[]{:S(2)}) copy-start(bf16[1,1,4,512,128]{4,3,2,1,0:T(8,128)(2,1)} %param.12) | copy-start | bytes 1572868
  236.6 49.6 %copy-start.1 = (bf16[1,1,4,128,512]{4,3,2,1,0:T(8,128)(2,1)S(1)}, bf16[1,1,4,128,512]{4,3,2,1,0:T(8,128)(2,1)}, u32[]{:S(2)}) copy-start(bf16[1,1,4,128,512]{4,3,2,1,0:T(8,128)(2,1)} %param.11) | copy-start | bytes 1572868
  238.6 46.1 %copy-start.4 = (bf16[384,128]{1,0:T(8,128)(2,1)S(1)}, bf16[384,128]{1,0:T(8,128)(2,1)}, u32[]{:S(2)}) copy-start(bf16[384,128]{1,0:T(8,128)(2,1)} %param.8) | copy-start | bytes 294916
  239.6 14.8 %collective-permute-start.7 = (bf16[4,384,128]{2,1,0:T(8,128)(2,1)S(1)}, bf16[4,384,128]{2,1,0:T(8,128)(2,1)S(1)}, u32[]{:S(2)}, u32[]{:S(2)}) collective-permute-start(bf16[4,384,128]{2,1,0:T(8,128)(2,1)S(1)} %get-tuple-element.19), channel_id=1, source_target_pairs={{0,1},{1,2},{2,3},{3,4},{4,5},{5,6},{6,7},{7,8},{8,9},{9,10},{10,1... | collective-permute-start | bytes 1179656 | tf_op jit(solution)/shard_map/ppermute | solution.py:13
  239.7 14.8 %collective-permute-start.6 = (bf16[4,384,128]{2,1,0:T(8,128)(2,1)S(1)}, bf16[4,384,128]{2,1,0:T(8,128)(2,1)S(1)}, u32[]{:S(2)}, u32[]{:S(2)}) collective-permute-start(bf16[4,384,128]{2,1,0:T(8,128)(2,1)S(1)} %get-tuple-element.18), channel_id=1, source_target_pairs={{0,31},{1,0},{2,1},{3,2},{4,3},{5,4},{6,5},{7,6},{8,7},{9,8},{10,9... | collective-permute-start | bytes 1179656 | tf_op jit(solution)/shard_map/ppermute | solution.py:13
Sparse Core Ops, SparseCore 0:
  255.5 29.1 reduce-scatter.1
where the time goes:
time: 298 us; the launch traced here: 293 us
  local copies, waits for them, and re-layouts  101 us (34%)
  other arithmetic  60.7 us (20%)
  matrix products  53.3 us (18%)
  waiting for transfers between devices  27.9 us (9%)
  starting transfers between devices  27 us (9%)
  between operations  14.5 us (5%)
  blocking collectives  8.57 us (3%)
    dot_general x2, matrix products, advance(): jnp.dot(mixing, rounded.reshape(channels, -1), preferred_element_type=jnp...  46.1 us
    reduce_sum x1, other arithmetic, shards(): row_sums = state.reshape(channels, rows // 4, 4, width).sum(axis=2)  38.8 us
    unnamed x25, local copies, waits for them, and re-layouts  32.5 us
    slice x2, local copies, waits for them, and re-layouts, laplace(): center = padded[:, 1:-1]  22.5 us
    reduce_scatter x1, waiting for transfers between devices, shards(): lax.psum_scatter(combined.astype(jnp.bfloat16), 'nest', scatter_dimension...  20.3 us
    convert_element_type x2, other arithmetic, shards(): with_halo(state.astype(jnp.bfloat16), (('tile', 1),), 1, False)  18.1 us
    mul x1, local copies, waits for them, and re-layouts, advance(): moved = state + factor[None] * (0.5 * mixed + laplace(padded))  12.6 us
    ppermute x3, starting transfers between devices, with_halo(): after = lax.ppermute(initial, axis, down)  10.5 us
  transfers between devices with their start and end apart: 9, of which 2 were waited for; matrix products, arithmetic and copies ran while one was open for 23% of the time, Pallas kernels for 0%

commit v1 on v0

v1 whole, which is shorter than its diff:
```python
import functools

import jax
import jax.numpy as jnp
from jax import lax
from jax.experimental import pallas as pl
from jax.experimental.pallas import tpu as pltpu
from jax.sharding import PartitionSpec as P

BW = 16
LANES = 128
MESH = pl.DeviceIdType.MESH
f32, bf16 = jnp.float32, jnp.bfloat16


def side_sum(x):
    zero = jnp.zeros((x.shape[0], 1), x.dtype)
    return jnp.concatenate([zero, x[:, :-1]], 1) + jnp.concatenate([x[:, 1:], zero], 1)


def kernel(
    groups, tiles, parts,
    picks, nest, parent, mix, interp, avg, land,
    nest_out, parent_out,
    xin, xa, xb, ws, cand, m_v, w_v, av_v, land_v, coef, strip_v, pool_v, coarse, fb, fbs, r1, s2, r2, s3, r3, g1, p_out,
    load_sem, p_send, p_recv, h_send, h_recv, f_send, f_recv, out_sem,
):
    channels, rows, width = xin.shape
    part = channels // parts
    slots = w_v.shape[0]
    n, t = lax.axis_index("nest"), lax.axis_index("tile")
    core = n + 1 - 2 * lax.rem(n, 2)
    deep = lax.rem(n + 2, groups)
    core_deep = lax.rem(core + 2, groups)
    up, down = lax.rem(t + 1, tiles), lax.rem(t + tiles - 1, tiles)
    to_up, to_down, to_core, to_deep = (n, up), (n, down), (core, t), (deep, t)

    def remote(src, dst, send, recv, device):
        return pltpu.make_async_remote_copy(
            src_ref=src, dst_ref=dst, send_sem=send, recv_sem=recv, device_id=device, device_id_type=MESH
        )

    barrier = pltpu.get_barrier_semaphore()
    for device in (to_up, to_down, to_core, to_deep):
        pl.semaphore_signal(barrier, inc=1, device_id=device, device_id_type=MESH)

    def span(c):
        return pl.ds(c * part, part)

    x_loads = [pltpu.make_async_copy(nest.at[0, span(c)], xin.at[span(c)], load_sem.at[c]) for c in range(parts)]
    own_load = pltpu.make_async_copy(parent, cand.at[3 * n + 1], load_sem.at[parts])
    mix_load = pltpu.make_async_copy(mix, m_v, load_sem.at[parts + 1])
    land_load = pltpu.make_async_copy(land.at[0], land_v, load_sem.at[parts + 2])
    w_load = pltpu.make_async_copy(interp.at[0, 0], w_v, load_sem.at[parts + 3])
    av_load = pltpu.make_async_copy(avg.at[0, 0], av_v, load_sem.at[parts + 4])
    own_load.start()
    for load in x_loads:
        load.start()
    for load in (mix_load, land_load, w_load, av_load):
        load.start()
    own_load.wait()
    pl.semaphore_wait(barrier, 4)

    own = cand.at[3 * n + 1]
    tile_up = remote(own, cand.at[3 * n], p_send.at[0], p_recv.at[0], to_up)
    tile_down = remote(own, cand.at[3 * n + 2], p_send.at[1], p_recv.at[1], to_down)
    tile_up.start()
    tile_down.start()

    def to_groups(o):
        mine = cand.at[3 * n + o]
        return (
            remote(mine, mine, p_send.at[2 + o], p_recv.at[2 + o], to_core),
            remote(mine, mine, p_send.at[5 + o], p_recv.at[5 + o], to_deep),
        )

    group_copies = [to_groups(o) for o in range(3)]
    for copy in group_copies[1]:
        copy.start()

    def halos(state, step, c):
        k = (step * parts + c) * 2
        return (
            remote(state.at[rows, span(c)], state.at[0, span(c)], h_send.at[k], h_recv.at[k], to_up),
            remote(state.at[1, span(c)], state.at[rows + 1, span(c)], h_send.at[k + 1], h_recv.at[k + 1], to_down),
        )

    def halo_start(state, step, c):
        upward, downward = halos(state, step, c)
        pl.when(t < tiles - 1)(upward.start)
        pl.when(t > 0)(downward.start)

    def halo_arrived(state, step, c):
        upward, downward = halos(state, step, c)
        pl.when(t > 0)(upward.wait_recv)
        pl.when(t < tiles - 1)(downward.wait_recv)

    def halo_sent(state, step, c):
        upward, downward = halos(state, step, c)
        pl.when(t < tiles - 1)(upward.wait_send)
        pl.when(t > 0)(downward.wait_send)

    @pl.when(t == 0)
    def _():
        for state in (xa, xb):
            state[0] = jnp.zeros((channels, width), bf16)

    @pl.when(t == tiles - 1)
    def _():
        for state in (xa, xb):
            state[rows + 1] = jnp.zeros((channels, width), bf16)

    for c in range(parts):
        x_loads[c].wait()

        def rows_first(i, carry, c=c):
            at = pl.ds(pl.multiple_of(c * part + i * 16, 16), 16)
            xa[1 : rows + 1, at, :] = jnp.swapaxes(xin[at], 0, 1)
            return carry

        lax.fori_loop(0, part // 16, rows_first, 0)
        halo_start(xa, 0, c)

    land_load.wait()
    mix_load.wait()
    column = lax.broadcasted_iota(jnp.int32, (rows, width), 1)
    edge = jnp.minimum(column, width - 1 - column)
    ramp = jnp.maximum(BW - edge, 0).astype(f32) / BW
    factor = jnp.where(land_v[...] == 1, 0.5, 1.0)
    coef[0] = (1.0 - ramp) * (1.0 - 0.9 * factor)
    coef[1] = (1.0 - ramp) * (0.4 * factor)

    tile_up.wait_recv()
    for copy in group_copies[0]:
        copy.start()
    tile_down.wait_recv()
    for copy in group_copies[2]:
        copy.start()

    def update(src, dst, r, first, count, with_strip):
        mixed = jnp.dot(m_v[first : first + count, :], src[r + 1], preferred_element_type=f32)
        mine, around = coef[0, pl.ds(r, 1), :], coef[1, pl.ds(r, 1), :]
        for s in range(0, count, 16):
            at = slice(first + s, first + s + 16)
            x = src[r + 1, at, :]
            near = src[r, at, :] + src[r + 2, at, :] + jnp.asarray(0.125, bf16) * side_sum(x)
            y = mine * x.astype(f32) + around * (near.astype(f32) + 1.25 * mixed[s : s + 16])
            if with_strip:
                west = y[:, :LANES] + ws[r, at, :LANES]
                east = y[:, -LANES:] + ws[r, at, LANES:]
                y = jnp.concatenate([west, y[:, LANES:-LANES], east], axis=1)
            dst[r + 1, at, :] = y.astype(bf16)

    def inner_rows(src, dst, with_strip):
        def body(i, carry):
            update(src, dst, 2 * i + 1, 0, channels, with_strip)
            update(src, dst, 2 * i + 2, 0, channels, with_strip)
            return carry

        lax.fori_loop(0, (rows - 2) // 2, body, 0)

    inner_rows(xa, xb, False)

    w_load.wait()
    for o in range(3):
        group_copies[o][1].wait_recv()
    theirs = cand.at[pl.ds(3 * deep, 3)]
    onward = remote(theirs, theirs, p_send.at[8], p_recv.at[8], to_core)
    onward.start()
    for o in range(3):
        group_copies[o][0].wait_recv()
    onward.wait_recv()
    picked = jnp.concatenate([cand[picks[0, 0, k]] for k in range(slots)], axis=1)
    weights = w_v[...].reshape(slots * LANES, width)
    strip_v[...] = jnp.dot(picked, weights, preferred_element_type=f32).astype(bf16)
    lane = lax.broadcasted_iota(jnp.int32, (1, LANES), 1)
    west_ramp = jnp.maximum(BW - lane, 0).astype(f32) / BW
    east_ramp = jnp.maximum(lane - (LANES - 1 - BW), 0).astype(f32) / BW
    per = LANES // (2 * BW)

    def spread(i, carry):
        at = pl.ds(pl.multiple_of(i * 16, 16), 16)
        for r in range(rows):
            cells = strip_v[at, (r // per) * LANES : (r // per + 1) * LANES].astype(f32)
            off = (r % per) * 2 * BW
            ws[r, at, :LANES] = pltpu.roll(cells, (LANES - off) % LANES, 1) * west_ramp
            ws[r, at, LANES:] = pltpu.roll(cells, (2 * LANES - 2 * BW - off) % LANES, 1) * east_ramp
        return carry

    lax.fori_loop(0, channels // 16, spread, 0)

    def add_strip(r, carry):
        for side, at in enumerate((slice(0, LANES), slice(width - LANES, width))):
            there = xb[r + 1, :, at].astype(f32) + ws[r, :, side * LANES : (side + 1) * LANES]
            xb[r + 1, :, at] = there.astype(bf16)
        return carry

    lax.fori_loop(1, rows - 1, add_strip, 0)

    for c in range(parts):
        halo_arrived(xa, 0, c)
        update(xa, xb, 0, c * part, part, True)
        update(xa, xb, rows - 1, c * part, part, True)
        halo_start(xb, 1, c)

    inner_rows(xb, xa, True)

    av_load.wait()
    pool_row = lax.broadcasted_iota(jnp.int32, (width, LANES), 0)
    pool_col = lax.broadcasted_iota(jnp.int32, (width, LANES), 1)
    pool_v[...] = jnp.where(pool_row // 4 == pool_col, 1.0 / 16.0, 0.0).astype(bf16)

    def average(b, first, count):
        at = slice(first, first + count)
        total = xa[4 * b + 1, at, :].astype(f32)
        for j in range(1, 4):
            total = total + xa[4 * b + 1 + j, at, :].astype(f32)
        blocks = jnp.dot(total.astype(bf16), pool_v[...], preferred_element_type=f32)
        coarse[at, b * LANES : (b + 1) * LANES] = blocks.astype(bf16)

    bands = rows // 4
    for b in range(1, bands - 1):
        average(b, 0, channels)
    for k in range(slots):
        fb[k] = jnp.dot(
            coarse[:, LANES : (bands - 1) * LANES],
            av_v[k, LANES : (bands - 1) * LANES, :],
            preferred_element_type=f32,
        )

    def core_copies(c):
        return (
            remote(fbs.at[c, core], r1.at[c, 0], f_send.at[5 * c], f_recv.at[5 * c], to_core),
            remote(fbs.at[c, core_deep], r1.at[c, 1], f_send.at[5 * c + 1], f_recv.at[5 * c + 1], to_core),
        )

    def deep_copy(c):
        return remote(s2.at[c], r2.at[c], f_send.at[5 * c + 2], f_recv.at[5 * c + 2], to_deep)

    def tile_copies(c):
        return (
            remote(s3.at[c, 0], r3.at[c, 0], f_send.at[5 * c + 3], f_recv.at[5 * c + 3], to_down),
            remote(s3.at[c, 1], r3.at[c, 1], f_send.at[5 * c + 4], f_recv.at[5 * c + 4], to_up),
        )

    def out_copy(c):
        return pltpu.make_async_copy(xin.at[span(c)], nest_out.at[0, span(c)], out_sem.at[c])

    def stage_core(c):
        for copy in core_copies(c):
            copy.wait_recv()
        s2[c] = (fbs[c, deep].astype(f32) + r1[c, 1].astype(f32)).astype(bf16)
        deep_copy(c).start()

    def stage_deep(c):
        deep_copy(c).wait_recv()
        total = fbs[c, n].astype(f32) + r1[c, 0].astype(f32) + r2[c].astype(f32)
        s3[c, 0] = total[0].astype(bf16)
        s3[c, 1] = total[2].astype(bf16)
        g1[c] = total[1]
        for copy in tile_copies(c):
            copy.start()

    def stage_tile(c):
        for copy in tile_copies(c):
            copy.wait_recv()
        mine = cand[3 * n + 1, span(c), :].astype(f32)
        total = mine + (g1[c] + r3[c, 0].astype(f32) + r3[c, 1].astype(f32))
        p_out[span(c), :] = total.astype(bf16)

    for c in range(parts):
        halo_sent(xa, 0, c)
        halo_arrived(xb, 1, c)
        update(xb, xa, 0, c * part, part, True)
        update(xb, xa, rows - 1, c * part, part, True)
        average(0, c * part, part)
        average(bands - 1, c * part, part)
        at = slice(c * part, (c + 1) * part)
        terms = []
        for k in range(slots):
            first = jnp.dot(coarse[at, :LANES], av_v[k, :LANES, :], preferred_element_type=f32)
            last = jnp.dot(
                coarse[at, (bands - 1) * LANES :], av_v[k, (bands - 1) * LANES :, :], preferred_element_type=f32
            )
            terms.append(fb[k, at, :] + first + last)
        for slot in range(3 * groups):
            total = jnp.zeros((part, LANES), f32)
            for k in range(slots):
                total = total + (picks[0, 0, k] == slot).astype(f32) * terms[k]
            fbs[c, slot // 3, slot % 3] = total.astype(bf16)
        for copy in core_copies(c):
            copy.start()
        if c > 0:
            stage_core(c - 1)

        def channels_first(i, carry, c=c):
            at = pl.ds(pl.multiple_of(c * part + i * 16, 16), 16)
            xin[at] = jnp.swapaxes(xa[1 : rows + 1, at, :], 0, 1)
            return carry

        lax.fori_loop(0, part // 16, channels_first, 0)
        out_copy(c).start()
        if c > 1:
            stage_deep(c - 2)
    stage_core(parts - 1)
    for c in range(parts - 2, parts):
        stage_deep(c)
    for c in range(parts):
        stage_tile(c)
    final = pltpu.make_async_copy(p_out, parent_out, load_sem.at[parts])
    final.start()

    tile_up.wait_send()
    tile_down.wait_send()
    for pair in group_copies:
        for copy in pair:
            copy.wait_send()
    onward.wait_send()
    for c in range(parts):
        halo_sent(xb, 1, c)
        for copy in core_copies(c):
            copy.wait_send()
        deep_copy(c).wait_send()
        for copy in tile_copies(c):
            copy.wait_send()
        out_copy(c).wait()
    final.wait()


def shards(nest_state, parent_state, mix_weight, intersection, interp_weight, avg_weight, land_mask):
    _, channels, rows, width = nest_state.shape
    groups, tiles = lax.axis_size("nest"), lax.axis_size("tile")
    slots = intersection.shape[2]
    cells = parent_state.shape[1]
    parts = 3
    part = channels // parts
    hbm = pl.BlockSpec(memory_space=pl.ANY)
    return pl.pallas_call(
        functools.partial(kernel, groups, tiles, parts),
        out_shape=(
            jax.ShapeDtypeStruct(nest_state.shape, bf16),
            jax.ShapeDtypeStruct(parent_state.shape, bf16),
        ),
        in_specs=[pl.BlockSpec(memory_space=pltpu.SMEM)] + [hbm] * 6,
        out_specs=(hbm, hbm),
        scratch_shapes=[
            pltpu.VMEM((channels, rows, width), bf16),
            pltpu.VMEM((rows + 2, channels, width), bf16),
            pltpu.VMEM((rows + 2, channels, width), bf16),
            pltpu.VMEM((rows, channels, 2 * LANES), f32),
            pltpu.VMEM((3 * groups, channels, cells), bf16),
            pltpu.VMEM((channels, channels), bf16),
            pltpu.VMEM((slots, cells, width), bf16),
            pltpu.VMEM((slots, width, cells), bf16),
            pltpu.VMEM((rows, width), jnp.int32),
            pltpu.VMEM((2, rows, width), f32),
            pltpu.VMEM((channels, width), bf16),
            pltpu.VMEM((width, LANES), bf16),
            pltpu.VMEM((channels, width), bf16),
            pltpu.VMEM((slots, channels, cells), f32),
            pltpu.VMEM((parts, groups, 3, part, cells), bf16),
            pltpu.VMEM((parts, 2, 3, part, cells), bf16),
            pltpu.VMEM((parts, 3, part, cells), bf16),
            pltpu.VMEM((parts, 3, part, cells), bf16),
            pltpu.VMEM((parts, 2, part, cells), bf16),
            pltpu.VMEM((parts, 2, part, cells), bf16),
            pltpu.VMEM((parts, part, cells), f32),
            pltpu.VMEM((channels, cells), bf16),
            pltpu.SemaphoreType.DMA((parts + 5,)),
            pltpu.SemaphoreType.DMA((9,)),
            pltpu.SemaphoreType.DMA((9,)),
            pltpu.SemaphoreType.DMA((4 * parts,)),
            pltpu.SemaphoreType.DMA((4 * parts,)),
            pltpu.SemaphoreType.DMA((5 * parts,)),
            pltpu.SemaphoreType.DMA((5 * parts,)),
            pltpu.SemaphoreType.DMA((parts,)),
        ],
        compiler_params=pltpu.CompilerParams(
            collective_id=0, has_side_effects=True, vmem_limit_bytes=56 * 2**20
        ),
    )(intersection, nest_state, parent_state, mix_weight, interp_weight, avg_weight, land_mask)


def solution(mesh):
    in_specs = (
        P("nest", None, "tile", None),
        P(None, ("nest", "tile")),
        P(),
        P("nest", "tile", None),
        P("nest", "tile", None, None, None),
        P("nest", "tile", None, None, None),
        P("nest", "tile", None),
    )
    out_specs = (P("nest", None, "tile", None), P(None, ("nest", "tile")))
    return jax.shard_map(shards, mesh=mesh, in_specs=in_specs, out_specs=out_specs, check_vma=False)
```

time: 298 us -> 65.6 us (0.22); the launches traced: 293 us -> 65.4 us
  local copies, waits for them, and re-layouts: 101 us -> 6.88 us
  other arithmetic: 60.7 us -> 0 us
  Pallas kernels: 0 us -> 57.9 us
  matrix products: 53.3 us -> 0 us
  waiting for transfers between devices: 27.9 us -> 0 us
  starting transfers between devices: 27 us -> 0 us
  between operations: 14.5 us -> 0.65 us
  blocking collectives: 8.57 us -> 0 us
    pallas_call x0 -> x1, Pallas kernels: none -> 57.9 us  [shards(): pl.pallas_call(functools.partial(kernel, groups, tiles, parts), out_shape...]
    dot_general x7 -> x0, matrix products: 53.3 us -> none  [the longest x2 46.1 us: advance(): jnp.dot(mixing, rounded.reshape(channels, -1), preferred_element_type=jnp...]
    reduce_sum x1 -> x0, other arithmetic: 38.8 us -> none  [shards(): row_sums = state.reshape(channels, rows // 4, 4, width).sum(axis=2)]
    ppermute x8 -> x0, starting transfers between devices: 27 us -> none  [the longest x3 10.5 us: with_halo(): after = lax.ppermute(initial, axis, down)]
    unnamed x25 -> x4, local copies, waits for them, and re-layouts: 32.5 us -> 6.88 us
    slice x5 -> x0, local copies, waits for them, and re-layouts: 24.6 us -> none  [the longest x2 22.5 us: laplace(): center = padded[:, 1:-1]]
    convert_element_type x4 -> x0, other arithmetic: 20.5 us -> none  [the longest x2 18.1 us: shards(): with_halo(state.astype(jnp.bfloat16), (('tile', 1),), 1, False)]
    reduce_scatter x1 -> x0, waiting for transfers between devices: 20.3 us -> none  [shards(): lax.psum_scatter(combined.astype(jnp.bfloat16), 'nest', scatter_dimension...]
  transfers between devices with their start and end apart: 9 -> 0, of which waited for: 2 -> 0; matrix products, arithmetic and copies ran while one was open for 23% -> 0% of each run, Pallas kernels for 0% -> 0%
where the time goes in v1:
time: 65.6 us; the launch traced here: 65.4 us
  Pallas kernels  57.9 us (88%)
  local copies, waits for them, and re-layouts  6.88 us (10%)
    pallas_call x1, Pallas kernels, shards(): pl.pallas_call(functools.partial(kernel, groups, tiles, parts), out_shape...  57.9 us
    unnamed x4, local copies, waits for them, and re-layouts  6.88 us

profile of v1, /device:TPU:1, one launch (start us, length us, event | category | flops | bytes accessed | tf_op | source)
XLA Modules:
  0.0 65.4 jit_solution(7570484258410064880)
XLA Ops:
  0.6 57.9 %shard_map.86 = (bf16[1,384,16,512]{3,2,1,0:T(8,128)(2,1)}, bf16[384,128]{1,0:T(8,128)(2,1)}) custom-call(s32[1,1,4]{2,1,0:T(1,128)} %picks.1, bf16[1,384,16,512]{3,2,1,0:T(8,128)(2,1)} %nest.1, bf16[384,128]{1,0:T(8,128)(2,1)} %parent.1, bf16[384,384]{1,0:T(8,128)(2,1)} %mix.1, bf16[1,1,4,128,512]{4,3,2,1,0:T(8,128)(2,1)} %interp.1, ...), custom_call_target="tpu_custom_call" | custom-call | tf_op jit(solution)/shard_map/pallas_call | solution.py:338
  58.5 0.0 copy-start
  58.6 6.2 %copy.11 = bf16[1,384,16,512]{3,2,1,0:T(8,128)(2,1)} copy(bf16[1,384,16,512]{3,2,1,0:T(8,128)(2,1)} %get-tuple-element.4) | data formatting | bytes 12582912
  64.8 0.0 copy-done
  64.8 0.6 copy.12
Async XLA Ops:
  58.5 6.2 %copy-start = (bf16[384,128]{1,0:T(8,128)(2,1)S(1)}, bf16[384,128]{1,0:T(8,128)(2,1)}, u32[]{:S(2)}) copy-start(bf16[384,128]{1,0:T(8,128)(2,1)} %get-tuple-element.5) | copy-start | bytes 294916

commit v2 on v1

v2 whole, which is shorter than its diff:
```python
import functools

import jax
import jax.numpy as jnp
from jax import lax
from jax.experimental import pallas as pl
from jax.experimental.pallas import tpu as pltpu
from jax.sharding import PartitionSpec as P

BW = 16
LANES = 128
MESH = pl.DeviceIdType.MESH
f32, bf16 = jnp.float32, jnp.bfloat16


def side_sum(x):
    zero = jnp.zeros((x.shape[0], 1), x.dtype)
    return jnp.concatenate([zero, x[:, :-1]], 1) + jnp.concatenate([x[:, 1:], zero], 1)


def kernel(
    groups, tiles, parts,
    picks, nest, parent, mix, interp, avg, land,
    x_out, p_out,
    xa, xb, xf, ws, cand, m_v, w_v, av_v, land_v, coef, strip_v, pack_v, ring_v, pool_v, tops, fb, fbs, r1, s2, r2, s3, r3, g1,
    load_sem, p_send, p_recv, h_send, h_recv, s_send, s_recv, f_send, f_recv,
):
    channels, rows, width = x_out.shape
    part = channels // parts
    slots = w_v.shape[0]
    bands = rows // 4
    n, t = lax.axis_index("nest"), lax.axis_index("tile")
    core = n + 1 - 2 * lax.rem(n, 2)
    deep = lax.rem(n + 2, groups)
    core_deep = lax.rem(core + 2, groups)
    up, down = lax.rem(t + 1, tiles), lax.rem(t + tiles - 1, tiles)
    to_up, to_down, to_core, to_deep = (n, up), (n, down), (core, t), (deep, t)
    first, last = t == 0, t == tiles - 1

    def remote(src, dst, send, recv, device):
        return pltpu.make_async_remote_copy(
            src_ref=src, dst_ref=dst, send_sem=send, recv_sem=recv, device_id=device, device_id_type=MESH
        )

    barrier = pltpu.get_barrier_semaphore()

    def greet(device):
        pl.semaphore_signal(barrier, inc=1, device_id=device, device_id_type=MESH)

    greet(to_core)
    greet(to_deep)
    pl.when(t < tiles - 1)(lambda: greet(to_up))
    pl.when(t > 0)(lambda: greet(to_down))

    def span(c):
        return pl.ds(c * part, part)

    x_loads = [pltpu.make_async_copy(nest.at[0, span(c)], x_out.at[span(c)], load_sem.at[c]) for c in range(parts)]
    own_load = pltpu.make_async_copy(parent, cand.at[3 * n + 1], load_sem.at[parts])
    mix_load = pltpu.make_async_copy(mix, m_v, load_sem.at[parts + 1])
    land_load = pltpu.make_async_copy(land.at[0], land_v, load_sem.at[parts + 2])
    w_load = pltpu.make_async_copy(interp.at[0, 0], w_v, load_sem.at[parts + 3])
    av_loads = [
        pltpu.make_async_copy(avg.at[0, 0, k], av_v.at[:, k * LANES : (k + 1) * LANES], load_sem.at[parts + 4 + k])
        for k in range(slots)
    ]
    own_load.start()
    for load in x_loads:
        load.start()
    for load in (mix_load, land_load, w_load, *av_loads):
        load.start()
    own_load.wait()

    @pl.when(first)
    def _():
        pl.semaphore_wait(barrier, 3)
        greet(to_down)

    @pl.when(t > 0)
    def _():
        pl.semaphore_wait(barrier, 4)

    pl.when(last)(lambda: greet(to_up))

    own = cand.at[3 * n + 1]
    tile_up = remote(own, cand.at[3 * n], p_send.at[0], p_recv.at[0], to_up)
    tile_down = remote(own, cand.at[3 * n + 2], p_send.at[1], p_recv.at[1], to_down)

    def to_groups(o):
        mine = cand.at[3 * n + o]
        return (
            remote(mine, mine, p_send.at[2 + o], p_recv.at[2 + o], to_core),
            remote(mine, mine, p_send.at[5 + o], p_recv.at[5 + o], to_deep),
        )

    group_copies = [to_groups(o) for o in range(3)]

    def from_below():
        tile_up.wait_recv()
        for copy in group_copies[0]:
            copy.start()

    def from_above():
        tile_down.wait_recv()
        for copy in group_copies[2]:
            copy.start()

    with jax.named_scope("own_tile"):
        tile_up.start()
        pl.when(t > 0)(tile_down.start)
        for copy in group_copies[1]:
            copy.start()

    def halos(state, step, c):
        k = (step * parts + c) * 2
        return (
            remote(state.at[rows, span(c)], state.at[0, span(c)], h_send.at[k], h_recv.at[k], to_up),
            remote(state.at[1, span(c)], state.at[rows + 1, span(c)], h_send.at[k + 1], h_recv.at[k + 1], to_down),
        )

    def halo_start(state, step, c):
        upward, downward = halos(state, step, c)
        pl.when(t < tiles - 1)(upward.start)
        pl.when(t > 0)(downward.start)

    def halo_arrived(state, step, c):
        upward, downward = halos(state, step, c)
        pl.when(t > 0)(upward.wait_recv)
        pl.when(t < tiles - 1)(downward.wait_recv)

    def halo_sent(state, step, c):
        upward, downward = halos(state, step, c)
        pl.when(t < tiles - 1)(upward.wait_send)
        pl.when(t > 0)(downward.wait_send)

    @pl.when(first)
    def _():
        ring_v[0] = jnp.zeros(ring_v.shape[1:], bf16)
        for state in (xa, xb):
            state[0] = jnp.zeros((channels, width), bf16)

    @pl.when(last)
    def _():
        ring_v[1] = jnp.zeros(ring_v.shape[1:], bf16)
        for state in (xa, xb):
            state[rows + 1] = jnp.zeros((channels, width), bf16)

    with jax.named_scope("rows_first"):
        for c in range(parts):
            x_loads[c].wait()

            def rows_first(i, carry, c=c):
                at = pl.ds(pl.multiple_of(c * part + i * 16, 16), 16)
                xa[1 : rows + 1, at, :] = jnp.swapaxes(x_out[at], 0, 1)
                return carry

            lax.fori_loop(0, part // 16, rows_first, 0)
            halo_start(xa, 0, c)

    land_load.wait()
    mix_load.wait()
    column = lax.broadcasted_iota(jnp.int32, (rows, width), 1)
    edge = jnp.minimum(column, width - 1 - column)
    ramp = jnp.maximum(BW - edge, 0).astype(f32) / BW
    factor = jnp.where(land_v[...] == 1, 0.5, 1.0)
    coef[0] = (1.0 - ramp) * (1.0 - 0.9 * factor)
    coef[1] = (1.0 - ramp) * (0.4 * factor)

    def new_value(x, above, below, sides, mixed, mine, around):
        near = above + below + jnp.asarray(0.125, bf16) * sides
        return mine * x.astype(f32) + around * (near.astype(f32) + 1.25 * mixed)

    def update(r, start, count):
        mixed = jnp.dot(m_v[start : start + count, :], xa[r + 1], preferred_element_type=f32)
        mine, around = coef[0, pl.ds(r, 1), :], coef[1, pl.ds(r, 1), :]
        for s in range(0, count, 16):
            at = slice(start + s, start + s + 16)
            x = xa[r + 1, at, :]
            y = new_value(x, xa[r, at, :], xa[r + 2, at, :], side_sum(x), mixed[s : s + 16], mine, around)
            xb[r + 1, at, :] = y.astype(bf16)

    def first_rows(begin, end):
        def body(i, carry):
            update(2 * i + 1, 0, channels)
            update(2 * i + 2, 0, channels)
            return carry

        lax.fori_loop(begin, end, body, 0)

    with jax.named_scope("first_inner"):
        first_rows(0, 2)
    with jax.named_scope("tile_on"):
        pl.when(t < tiles - 1)(from_above)
        pl.when(last)(from_below)
    with jax.named_scope("first_inner"):
        first_rows(2, (rows - 2) // 2)

    @pl.when(first)
    def _():
        pl.semaphore_wait(barrier, 1)
        tile_down.start()

    for c in range(parts):
        with jax.named_scope("first_halo_wait"):
            halo_arrived(xa, 0, c)
        with jax.named_scope("first_edges"):
            update(0, c * part, part)
            update(rows - 1, c * part, part)
        if c < parts - 1:
            halo_start(xb, 1, c)

    with jax.named_scope("tile_on"):
        pl.when(t < tiles - 1)(from_below)
        pl.when(last)(from_above)

    mid, low, high = slice(LANES, width - LANES), slice(0, LANES), slice(width - LANES, width)

    def update_mid(r, start, count):
        mixed = jnp.dot(m_v[start : start + count, :], xb[r + 1, :, mid], preferred_element_type=f32)
        mine, around = coef[0, pl.ds(r, 1), :][:, mid], coef[1, pl.ds(r, 1), :][:, mid]
        for s in range(0, count, 16):
            at = slice(start + s, start + s + 16)
            x = xb[r + 1, at, :]
            sides = side_sum(x)[:, mid]
            y = new_value(x[:, mid], xb[r, at, mid], xb[r + 2, at, mid], sides, mixed[s : s + 16], mine, around)
            xa[r + 1, at, mid] = y.astype(bf16)

    def update_out(r, start, count):
        mixed = jnp.dot(m_v[start : start + count, :], xf[r + 1], preferred_element_type=f32)
        mine, around = [
            jnp.concatenate([row[:, low], row[:, high]], axis=1) for row in (coef[0, pl.ds(r, 1), :], coef[1, pl.ds(r, 1), :])
        ]
        for s in range(0, count, 16):
            at = slice(start + s, start + s + 16)
            x = xf[r + 1, at, :]
            whole = side_sum(jnp.concatenate([x[:, :LANES], xb[r + 1, at, mid], x[:, LANES:]], axis=1))
            sides = jnp.concatenate([whole[:, low], whole[:, high]], axis=1)
            y = new_value(x, xf[r, at, :], xf[r + 2, at, :], sides, mixed[s : s + 16], mine, around)
            y = (y + ws[r, at, :]).astype(bf16)
            xa[r + 1, at, low] = y[:, :LANES]
            xa[r + 1, at, high] = y[:, LANES:]

    def inner_rows(one_row):
        def body(i, carry):
            one_row(2 * i + 1, 0, channels)
            one_row(2 * i + 2, 0, channels)
            return carry

        lax.fori_loop(0, (rows - 2) // 2, body, 0)

    for c in range(parts):
        halo_sent(xa, 0, c)
    with jax.named_scope("second_middle"):
        inner_rows(update_mid)

    w_load.wait()
    with jax.named_scope("deep_tiles_wait"):
        for o in range(3):
            group_copies[o][1].wait_recv()
    theirs = cand.at[pl.ds(3 * deep, 3)]
    onward = remote(theirs, theirs, p_send.at[8], p_recv.at[8], to_core)
    onward.start()
    with jax.named_scope("core_tiles_wait"):
        for o in range(3):
            group_copies[o][0].wait_recv()
        onward.wait_recv()
    with jax.named_scope("strip"):
        picked = jnp.concatenate([cand[picks[0, 0, k]] for k in range(slots)], axis=1)
        weights = w_v[...].reshape(slots * LANES, width)
        strip_v[...] = jnp.dot(picked, weights, preferred_element_type=f32).astype(bf16)

    cells = 2 * BW
    per = LANES // cells
    short = channels // per

    def pack(begin):
        return jnp.concatenate([strip_v[q * short : (q + 1) * short, begin : begin + cells] for q in range(per)], axis=1)

    ring_up = remote(pack_v.at[0], ring_v.at[0], s_send.at[0], s_recv.at[0], to_up)
    ring_down = remote(pack_v.at[1], ring_v.at[1], s_send.at[1], s_recv.at[1], to_down)
    with jax.named_scope("strip_send"):
        pack_v[0] = pack(width - cells)
        pack_v[1] = pack(0)
        pl.when(t < tiles - 1)(ring_up.start)
        pl.when(t > 0)(ring_down.start)
        halo_start(xb, 1, parts - 1)

    lane = lax.broadcasted_iota(jnp.int32, (1, LANES), 1)
    west_ramp = jnp.maximum(BW - lane, 0).astype(f32) / BW
    east_ramp = jnp.maximum(lane - (LANES - 1 - BW), 0).astype(f32) / BW

    def west_of(value, off):
        return pltpu.roll(value, (LANES - off) % LANES, 1) * west_ramp

    def east_of(value, off):
        return pltpu.roll(value, (2 * LANES - BW - BW - off) % LANES, 1) * east_ramp

    def spread(i, carry):
        at = pl.ds(pl.multiple_of(i * 16, 16), 16)
        for r in range(rows):
            value = strip_v[at, (r // per) * LANES : (r // per + 1) * LANES].astype(f32)
            off = (r % per) * cells
            west, east = west_of(value, off), east_of(value, off)
            ws[r, at, :LANES] = west
            ws[r, at, LANES:] = east
            xf[r + 1, at, :LANES] = (xb[r + 1, at, low].astype(f32) + west).astype(bf16)
            xf[r + 1, at, LANES:] = (xb[r + 1, at, high].astype(f32) + east).astype(bf16)
        return carry

    with jax.named_scope("strip_spread"):
        lax.fori_loop(0, channels // 16, spread, 0)

    with jax.named_scope("second_outer"):
        inner_rows(update_out)

    for load in av_loads:
        load.wait()
    pool_row = lax.broadcasted_iota(jnp.int32, (width, LANES), 0)
    pool_col = lax.broadcasted_iota(jnp.int32, (width, LANES), 1)
    pool_v[...] = jnp.where(pool_row // 4 == pool_col, 1.0 / 16.0, 0.0).astype(bf16)

    def row_total(begin, count, at):
        total = xa[begin + 1, at, :].astype(f32)
        for j in range(1, count):
            total = total + xa[begin + 1 + j, at, :].astype(f32)
        return total

    def averaged(total):
        return jnp.dot(total.astype(bf16), pool_v[...], preferred_element_type=f32).astype(bf16)

    everything = slice(0, channels)
    with jax.named_scope("feedback_inner"):
        tops[0] = row_total(1, 3, everything)
        tops[1] = row_total(rows - 4, 3, everything)
        middle = jnp.concatenate([averaged(row_total(4 * b, 4, everything)) for b in range(1, bands - 1)], axis=1)
        fb[...] = jnp.dot(middle, av_v[LANES : (bands - 1) * LANES, :], preferred_element_type=f32)

    def core_copies(c):
        return (
            remote(fbs.at[c, core], r1.at[c, 0], f_send.at[5 * c], f_recv.at[5 * c], to_core),
            remote(fbs.at[c, core_deep], r1.at[c, 1], f_send.at[5 * c + 1], f_recv.at[5 * c + 1], to_core),
        )

    def deep_copy(c):
        return remote(s2.at[c], r2.at[c], f_send.at[5 * c + 2], f_recv.at[5 * c + 2], to_deep)

    def tile_copies(c):
        return (
            remote(s3.at[c, 0], r3.at[c, 0], f_send.at[5 * c + 3], f_recv.at[5 * c + 3], to_down),
            remote(s3.at[c, 1], r3.at[c, 1], f_send.at[5 * c + 4], f_recv.at[5 * c + 4], to_up),
        )

    def stage_core(c):
        for copy in core_copies(c):
            copy.wait_recv()
        s2[c] = (fbs[c, deep].astype(f32) + r1[c, 1].astype(f32)).astype(bf16)
        deep_copy(c).start()

    def stage_deep(c):
        deep_copy(c).wait_recv()
        total = fbs[c, n].astype(f32) + r1[c, 0].astype(f32) + r2[c].astype(f32)
        s3[c, 0] = total[0].astype(bf16)
        s3[c, 1] = total[2].astype(bf16)
        g1[c] = total[1]
        for copy in tile_copies(c):
            copy.start()

    def stage_tile(c):
        for copy in tile_copies(c):
            copy.wait_recv()
        mine = cand[3 * n + 1, span(c), :].astype(f32)
        total = mine + (g1[c] + r3[c, 0].astype(f32) + r3[c, 1].astype(f32))
        p_out[span(c), :] = total.astype(bf16)

    def channels_first(c):
        def body(i, carry):
            at = pl.ds(pl.multiple_of(c * part + i * 16, 16), 16)
            x_out[at] = jnp.swapaxes(xa[1 : rows + 1, at, :], 0, 1)
            return carry

        lax.fori_loop(0, part // 16, body, 0)

    with jax.named_scope("strip_wait"):
        pl.when(t > 0)(ring_up.wait_recv)
        pl.when(t < tiles - 1)(ring_down.wait_recv)

    def halo_strip(c):
        for side, row in ((0, 0), (1, rows + 1)):
            for q in range(per):
                begin, end = max(q * short, c * part), min((q + 1) * short, (c + 1) * part)
                if begin < end:
                    at = slice(begin, end)
                    value = ring_v[side, begin - q * short : end - q * short, :].astype(f32)
                    xf[row, at, :LANES] = (xb[row, at, low].astype(f32) + west_of(value, q * cells)).astype(bf16)
                    xf[row, at, LANES:] = (xb[row, at, high].astype(f32) + east_of(value, q * cells)).astype(bf16)

    for c in range(parts):
        with jax.named_scope("second_halo_wait"):
            halo_arrived(xb, 1, c)
        with jax.named_scope("second_edges"):
            halo_strip(c)
            for r in (0, rows - 1):
                update_mid(r, c * part, part)
                update_out(r, c * part, part)
        at = slice(c * part, (c + 1) * part)
        with jax.named_scope("feedback_edges"):
            low_band = averaged(tops[0, at, :] + xa[1, at, :].astype(f32))
            high_band = averaged(tops[1, at, :] + xa[rows, at, :].astype(f32))
            terms = fb[at, :] + jnp.dot(low_band, av_v[:LANES, :], preferred_element_type=f32)
            terms = terms + jnp.dot(high_band, av_v[(bands - 1) * LANES :, :], preferred_element_type=f32)
        with jax.named_scope("feedback_slots"):
            for slot in range(3 * groups):
                total = jnp.zeros((part, LANES), f32)
                for k in range(slots):
                    total = total + (picks[0, 0, k] == slot).astype(f32) * terms[:, k * LANES : (k + 1) * LANES]
                fbs[c, slot // 3, slot % 3] = total.astype(bf16)
            for copy in core_copies(c):
                copy.start()
        if c > 0:
            with jax.named_scope("feedback_core"):
                stage_core(c - 1)
    with jax.named_scope("channels_first"):
        channels_first(0)
    with jax.named_scope("feedback_core"):
        stage_core(parts - 1)
    with jax.named_scope("channels_first"):
        for c in range(1, parts):
            channels_first(c)
    for c in range(parts):
        with jax.named_scope("feedback_deep"):
            stage_deep(c)
    for c in range(parts):
        with jax.named_scope("feedback_tile"):
            stage_tile(c)

    with jax.named_scope("sent"):
        tile_up.wait_send()
        tile_down.wait_send()
        for pair in group_copies:
            for copy in pair:
                copy.wait_send()
        onward.wait_send()
        pl.when(t < tiles - 1)(ring_up.wait_send)
        pl.when(t > 0)(ring_down.wait_send)
        for c in range(parts):
            halo_sent(xb, 1, c)
            for copy in core_copies(c):
                copy.wait_send()
            deep_copy(c).wait_send()
            for copy in tile_copies(c):
                copy.wait_send()


def write_out(x, p, nest_out, parent_out, sem):
    copies = [
        pltpu.make_async_copy(x, nest_out.at[0], sem.at[0]),
        pltpu.make_async_copy(p, parent_out, sem.at[1]),
    ]
    for copy in copies:
        copy.start()
    for copy in copies:
        copy.wait()


def shards(nest_state, parent_state, mix_weight, intersection, interp_weight, avg_weight, land_mask):
    _, channels, rows, width = nest_state.shape
    groups, tiles = lax.axis_size("nest"), lax.axis_size("tile")
    slots = intersection.shape[2]
    cells = parent_state.shape[1]
    parts = 3
    part = channels // parts
    hbm = pl.BlockSpec(memory_space=pl.ANY)
    vmem = pl.BlockSpec(memory_space=pltpu.VMEM)
    x_new, p_new = pl.pallas_call(
        functools.partial(kernel, groups, tiles, parts),
        out_shape=(pltpu.VMEM((channels, rows, width), bf16), pltpu.VMEM((channels, cells), bf16)),
        in_specs=[pl.BlockSpec(memory_space=pltpu.SMEM)] + [hbm] * 6,
        out_specs=(vmem, vmem),
        scratch_shapes=[
            pltpu.VMEM((rows + 2, channels, width), bf16),
            pltpu.VMEM((rows + 2, channels, width), bf16),
            pltpu.VMEM((rows + 2, channels, 2 * LANES), bf16),
            pltpu.VMEM((rows, channels, 2 * LANES), f32),
            pltpu.VMEM((3 * groups, channels, cells), bf16),
            pltpu.VMEM((channels, channels), bf16),
            pltpu.VMEM((slots, cells, width), bf16),
            pltpu.VMEM((width, slots * cells), bf16),
            pltpu.VMEM((rows, width), jnp.int32),
            pltpu.VMEM((2, rows, width), f32),
            pltpu.VMEM((channels, width), bf16),
            pltpu.VMEM((2, channels * 2 * BW // LANES, LANES), bf16),
            pltpu.VMEM((2, channels * 2 * BW // LANES, LANES), bf16),
            pltpu.VMEM((width, LANES), bf16),
            pltpu.VMEM((2, channels, width), f32),
            pltpu.VMEM((channels, slots * cells), f32),
            pltpu.VMEM((parts, groups, 3, part, cells), bf16),
            pltpu.VMEM((parts, 2, 3, part, cells), bf16),
            pltpu.VMEM((parts, 3, part, cells), bf16),
            pltpu.VMEM((parts, 3, part, cells), bf16),
            pltpu.VMEM((parts, 2, part, cells), bf16),
            pltpu.VMEM((parts, 2, part, cells), bf16),
            pltpu.VMEM((parts, part, cells), f32),
            pltpu.SemaphoreType.DMA((parts + 4 + slots,)),
            pltpu.SemaphoreType.DMA((9,)),
            pltpu.SemaphoreType.DMA((9,)),
            pltpu.SemaphoreType.DMA((4 * parts,)),
            pltpu.SemaphoreType.DMA((4 * parts,)),
            pltpu.SemaphoreType.DMA((2,)),
            pltpu.SemaphoreType.DMA((2,)),
            pltpu.SemaphoreType.DMA((5 * parts,)),
            pltpu.SemaphoreType.DMA((5 * parts,)),
        ],
        compiler_params=pltpu.CompilerParams(
            collective_id=0, has_side_effects=True, vmem_limit_bytes=48 * 2**20
        ),
    )(intersection, nest_state, parent_state, mix_weight, interp_weight, avg_weight, land_mask)
    return pl.pallas_call(
        write_out,
        out_shape=(
            jax.ShapeDtypeStruct(nest_state.shape, bf16),
            jax.ShapeDtypeStruct(parent_state.shape, bf16),
        ),
        in_specs=[vmem, vmem],
        out_specs=(hbm, hbm),
        scratch_shapes=[pltpu.SemaphoreType.DMA((2,))],
    )(x_new, p_new)


def solution(mesh):
    in_specs = (
        P("nest", None, "tile", None),
        P(None, ("nest", "tile")),
        P(),
        P("nest", "tile", None),
        P("nest", "tile", None, None, None),
        P("nest", "tile", None, None, None),
        P("nest", "tile", None),
    )
    out_specs = (P("nest", None, "tile", None), P(None, ("nest", "tile")))
    return jax.shard_map(shards, mesh=mesh, in_specs=in_specs, out_specs=out_specs, check_vma=False)
```

time: 65.6 us -> 71 us (1.082)
  the two profiles are of different devices: /device:TPU:1 before, /device:TPU:32 now
where the time goes in v2:
time: 71 us; the launch traced here: 70.8 us
  Pallas kernels  66.9 us (94%)
  local copies, waits for them, and re-layouts  3.28 us (5%)
    pallas_call x1, Pallas kernels, shards(): pl.pallas_call(functools.partial(kernel, groups, tiles, parts), out_shape...  61.4 us
    pallas_call x1, Pallas kernels, shards(): pl.pallas_call(write_out, out_shape=(jax.ShapeDtypeStruct(nest_state.shap...  5.51 us
    unnamed x4, local copies, waits for them, and re-layouts  3.28 us

profile of v2, /device:TPU:32, one launch (start us, length us, event | category | flops | bytes accessed | tf_op | source)
XLA Modules:
  0.0 70.8 jit_solution(13732702277309995719)
XLA Ops:
  0.6 61.4 %shard_map.86 = (bf16[384,16,512]{2,1,0:T(8,128)(2,1)S(1)}, bf16[384,128]{1,0:T(8,128)(2,1)S(1)}) custom-call(s32[1,1,4]{2,1,0:T(1,128)} %picks.1, bf16[1,384,16,512]{3,2,1,0:T(8,128)(2,1)} %nest.1, bf16[384,128]{1,0:T(8,128)(2,1)} %parent.1, bf16[384,384]{1,0:T(8,128)(2,1)} %mix.1, bf16[1,1,4,128,512]{4,3,2,1,0:T(8,128)(2,1)} %interp.1, ...), custom_call_target="tpu_custom_call" | custom-call | tf_op jit(solution)/shard_map/pallas_call | solution.py:474
  62.0 0.0 copy-start
  62.0 2.6 %copy-done = bf16[384,16,512]{2,1,0:T(8,128)(2,1)} copy-done((bf16[384,16,512]{2,1,0:T(8,128)(2,1)}, bf16[384,16,512]{2,1,0:T(8,128)(2,1)S(1)}, u32[]{:S(2)}) %copy-start) | copy-done | bytes 6291480
  64.7 0.0 copy-start.1
  64.7 0.6 copy-done.1
  65.3 5.5 %shard_map.87 = (bf16[1,384,16,512]{3,2,1,0:T(8,128)(2,1)}, bf16[384,128]{1,0:T(8,128)(2,1)}) custom-call(bf16[384,16,512]{2,1,0:T(8,128)(2,1)} %copy-done, bf16[384,128]{1,0:T(8,128)(2,1)} %copy-done.1), custom_call_target="tpu_custom_call" | custom-call | tf_op jit(solution)/shard_map/pallas_call | solution.py:517
Async XLA Ops:
  62.0 2.6 %copy-start = (bf16[384,16,512]{2,1,0:T(8,128)(2,1)}, bf16[384,16,512]{2,1,0:T(8,128)(2,1)S(1)}, u32[]{:S(2)}) copy-start(bf16[384,16,512]{2,1,0:T(8,128)(2,1)S(1)} %get-tuple-element.4.x) | copy-start | bytes 18874372
  64.7 0.6 copy-start.1

commit v3 on v2

--- a/solution.py
+++ b/solution.py
@@ -22,7 +22,7 @@
     groups, tiles, parts,
     picks, nest, parent, mix, interp, avg, land,
     x_out, p_out,
-    xa, xb, xf, ws, cand, m_v, w_v, av_v, land_v, coef, strip_v, pack_v, ring_v, pool_v, tops, fb, fbs, r1, s2, r2, s3, r3, g1,
+    xa, xb, xf, ws, cand, m_v, w_v, av_v, land_v, coef, strip_v, place_v, pack_v, ring_v, pool_v, tops, fb, fbs, r1, s2, r2, s3, r3, g1,
     load_sem, p_send, p_recv, h_send, h_recv, s_send, s_recv, f_send, f_recv,
 ):
     channels, rows, width = x_out.shape
@@ -36,6 +36,8 @@
     up, down = lax.rem(t + 1, tiles), lax.rem(t + tiles - 1, tiles)
     to_up, to_down, to_core, to_deep = (n, up), (n, down), (core, t), (deep, t)
     first, last = t == 0, t == tiles - 1
+    inside = jnp.logical_and(t > 0, t < tiles - 1)
+    ends = jnp.logical_or(first, last)
 
     def remote(src, dst, send, recv, device):
         return pltpu.make_async_remote_copy(
@@ -75,12 +77,17 @@
     def _():
         pl.semaphore_wait(barrier, 3)
         greet(to_down)
-
-    @pl.when(t > 0)
+        greet((deep, down))
+
+    @pl.when(inside)
     def _():
         pl.semaphore_wait(barrier, 4)
 
-    pl.when(last)(lambda: greet(to_up))
+    @pl.when(last)
+    def _():
+        pl.semaphore_wait(barrier, 5)
+        greet(to_up)
+        greet((deep, up))
 
     own = cand.at[3 * n + 1]
     tile_up = remote(own, cand.at[3 * n], p_send.at[0], p_recv.at[0], to_up)
@@ -95,19 +102,28 @@
 
     group_copies = [to_groups(o) for o in range(3)]
 
+    over_up = remote(own, cand.at[3 * n], p_send.at[9], p_recv.at[9], (deep, up))
+    over_down = remote(own, cand.at[3 * n + 2], p_send.at[9], p_recv.at[9], (deep, down))
+    deep_own = cand.at[3 * deep + 1]
+    beside_down = remote(deep_own, cand.at[3 * deep + 2], p_send.at[10], p_recv.at[10], to_down)
+    beside_up = remote(deep_own, cand.at[3 * deep], p_send.at[10], p_recv.at[10], to_up)
+
+    def pass_on(o):
+        group_copies[o][0].start()
+        pl.when(inside)(group_copies[o][1].start)
+
     def from_below():
         tile_up.wait_recv()
-        for copy in group_copies[0]:
-            copy.start()
+        pass_on(0)
 
     def from_above():
         tile_down.wait_recv()
-        for copy in group_copies[2]:
-            copy.start()
+        pass_on(2)
 
     with jax.named_scope("own_tile"):
         tile_up.start()
         pl.when(t > 0)(tile_down.start)
+        pl.when(last)(over_up.start)
         for copy in group_copies[1]:
             copy.start()
 
@@ -156,6 +172,15 @@
 
             lax.fori_loop(0, part // 16, rows_first, 0)
             halo_start(xa, 0, c)
+
+    source = lax.broadcasted_iota(jnp.int32, (LANES, 2 * LANES), 0)
+    target = lax.broadcasted_iota(jnp.int32, (LANES, 2 * LANES), 1)
+    west_at = jnp.where(target < BW, target, -LANES)
+    east_at = jnp.where(target >= 2 * LANES - BW, target - (2 * LANES - 2 * BW), -LANES)
+    weight = jnp.where(target < BW, BW - target, target - (2 * LANES - BW - 1)).astype(f32) / BW
+    for j in range(LANES // (2 * BW)):
+        here = source - j * 2 * BW
+        place_v[j] = jnp.where((here == west_at) | (here == east_at), weight, 0.0).astype(bf16)
 
     land_load.wait()
     mix_load.wait()
@@ -188,30 +213,13 @@
         lax.fori_loop(begin, end, body, 0)
 
     with jax.named_scope("first_inner"):
-        first_rows(0, 2)
+        first_rows(0, (rows - 2) // 2)
     with jax.named_scope("tile_on"):
         pl.when(t < tiles - 1)(from_above)
-        pl.when(last)(from_below)
-    with jax.named_scope("first_inner"):
-        first_rows(2, (rows - 2) // 2)
-
-    @pl.when(first)
-    def _():
-        pl.semaphore_wait(barrier, 1)
-        tile_down.start()
-
-    for c in range(parts):
-        with jax.named_scope("first_halo_wait"):
-            halo_arrived(xa, 0, c)
-        with jax.named_scope("first_edges"):
-            update(0, c * part, part)
-            update(rows - 1, c * part, part)
-        if c < parts - 1:
-            halo_start(xb, 1, c)
-
-    with jax.named_scope("tile_on"):
-        pl.when(t < tiles - 1)(from_below)
-        pl.when(last)(from_above)
+        pl.when(t > 0)(from_below)
+        group_copies[1][1].wait_recv()
+        pl.when(t == 1)(beside_down.start)
+        pl.when(t == tiles - 2)(beside_up.start)
 
     mid, low, high = slice(LANES, width - LANES), slice(0, LANES), slice(width - LANES, width)
 
@@ -236,27 +244,63 @@
             whole = side_sum(jnp.concatenate([x[:, :LANES], xb[r + 1, at, mid], x[:, LANES:]], axis=1))
             sides = jnp.concatenate([whole[:, low], whole[:, high]], axis=1)
             y = new_value(x, xf[r, at, :], xf[r + 2, at, :], sides, mixed[s : s + 16], mine, around)
-            y = (y + ws[r, at, :]).astype(bf16)
+            y = (y + ws[r, at, :].astype(f32)).astype(bf16)
             xa[r + 1, at, low] = y[:, :LANES]
             xa[r + 1, at, high] = y[:, LANES:]
 
-    def inner_rows(one_row):
+    def pairs(one_row, begin, end):
         def body(i, carry):
+            one_row(2 * i, 0, channels)
             one_row(2 * i + 1, 0, channels)
-            one_row(2 * i + 2, 0, channels)
             return carry
 
-        lax.fori_loop(0, (rows - 2) // 2, body, 0)
-
+        lax.fori_loop(begin // 2, end // 2, body, 0)
+
+    stops = [2 + 2 * ((rows - 4) // 2 * c // parts) for c in range(parts + 1)]
     for c in range(parts):
-        halo_sent(xa, 0, c)
+        with jax.named_scope("first_halo_wait"):
+            halo_arrived(xa, 0, c)
+        with jax.named_scope("first_edges"):
+            update(0, c * part, part)
+            update(rows - 1, c * part, part)
+        if c < parts - 1:
+            halo_start(xb, 1, c)
+            with jax.named_scope("second_middle"):
+                pairs(update_mid, stops[c], stops[c + 1])
+        if c == 1:
+
+            @pl.when(first)
+            def _():
+                pl.semaphore_wait(barrier, 2)
+                tile_down.start()
+                over_down.start()
+
+    with jax.named_scope("tile_on"):
+        pl.when(first)(from_below)
+        pl.when(last)(from_above)
     with jax.named_scope("second_middle"):
-        inner_rows(update_mid)
+        pairs(update_mid, stops[parts - 1], stops[parts])
+        update_mid(1, 0, channels)
+        update_mid(rows - 2, 0, channels)
 
     w_load.wait()
     with jax.named_scope("deep_tiles_wait"):
-        for o in range(3):
-            group_copies[o][1].wait_recv()
+
+        @pl.when(inside)
+        def _():
+            group_copies[0][1].wait_recv()
+            group_copies[2][1].wait_recv()
+
+        @pl.when(first)
+        def _():
+            over_up.wait_recv()
+            beside_down.wait_recv()
+
+        @pl.when(last)
+        def _():
+            over_down.wait_recv()
+            beside_up.wait_recv()
+
     theirs = cand.at[pl.ds(3 * deep, 3)]
     onward = remote(theirs, theirs, p_send.at[8], p_recv.at[8], to_core)
     onward.start()
@@ -285,33 +329,28 @@
         pl.when(t > 0)(ring_down.start)
         halo_start(xb, 1, parts - 1)
 
-    lane = lax.broadcasted_iota(jnp.int32, (1, LANES), 1)
-    west_ramp = jnp.maximum(BW - lane, 0).astype(f32) / BW
-    east_ramp = jnp.maximum(lane - (LANES - 1 - BW), 0).astype(f32) / BW
-
-    def west_of(value, off):
-        return pltpu.roll(value, (LANES - off) % LANES, 1) * west_ramp
-
-    def east_of(value, off):
-        return pltpu.roll(value, (2 * LANES - BW - BW - off) % LANES, 1) * east_ramp
-
-    def spread(i, carry):
-        at = pl.ds(pl.multiple_of(i * 16, 16), 16)
-        for r in range(rows):
-            value = strip_v[at, (r // per) * LANES : (r // per + 1) * LANES].astype(f32)
-            off = (r % per) * cells
-            west, east = west_of(value, off), east_of(value, off)
-            ws[r, at, :LANES] = west
-            ws[r, at, LANES:] = east
-            xf[r + 1, at, :LANES] = (xb[r + 1, at, low].astype(f32) + west).astype(bf16)
-            xf[r + 1, at, LANES:] = (xb[r + 1, at, high].astype(f32) + east).astype(bf16)
+    def placed(value, j):
+        return jnp.dot(value, place_v[j], preferred_element_type=f32)
+
+    def fixed(row, at, wide):
+        xf[row, at, :LANES] = (xb[row, at, low].astype(f32) + wide[:, :LANES]).astype(bf16)
+        xf[row, at, LANES:] = (xb[row, at, high].astype(f32) + wide[:, LANES:]).astype(bf16)
+
+    def spread(b, carry):
+        value = strip_v[:, pl.ds(pl.multiple_of(b * LANES, LANES), LANES)]
+        for j in range(per):
+            wide = placed(value, j)
+            ws[per * b + j] = wide.astype(bf16)
+            fixed(per * b + j + 1, slice(0, channels), wide)
         return carry
 
     with jax.named_scope("strip_spread"):
-        lax.fori_loop(0, channels // 16, spread, 0)
+        lax.fori_loop(0, rows // per, spread, 0)
 
     with jax.named_scope("second_outer"):
-        inner_rows(update_out)
+        update_out(1, 0, channels)
+        update_out(rows - 2, 0, channels)
+        pairs(update_out, 2, rows - 2)
 
     for load in av_loads:
         load.wait()
@@ -390,10 +429,10 @@
                 begin, end = max(q * short, c * part), min((q + 1) * short, (c + 1) * part)
                 if begin < end:
                     at = slice(begin, end)
-                    value = ring_v[side, begin - q * short : end - q * short, :].astype(f32)
-                    xf[row, at, :LANES] = (xb[row, at, low].astype(f32) + west_of(value, q * cells)).astype(bf16)
-                    xf[row, at, LANES:] = (xb[row, at, high].astype(f32) + east_of(value, q * cells)).astype(bf16)
-
+                    fixed(row, at, placed(ring_v[side, begin - q * short : end - q * short, :], q))
+
+    for c in range(parts):
+        halo_sent(xa, 0, c)
     for c in range(parts):
         with jax.named_scope("second_halo_wait"):
             halo_arrived(xb, 1, c)
@@ -436,9 +475,17 @@
     with jax.named_scope("sent"):
         tile_up.wait_send()
         tile_down.wait_send()
-        for pair in group_copies:
-            for copy in pair:
-                copy.wait_send()
+        for copy, _ in group_copies:
+            copy.wait_send()
+        group_copies[1][1].wait_send()
+
+        @pl.when(inside)
+        def _():
+            group_copies[0][1].wait_send()
+            group_copies[2][1].wait_send()
+
+        pl.when(ends)(over_up.wait_send)
+        pl.when(jnp.logical_or(t == 1, t == tiles - 2))(beside_up.wait_send)
         onward.wait_send()
         pl.when(t < tiles - 1)(ring_up.wait_send)
         pl.when(t > 0)(ring_down.wait_send)
@@ -451,11 +498,12 @@
                 copy.wait_send()
 
 
-def write_out(x, p, nest_out, parent_out, sem):
-    copies = [
-        pltpu.make_async_copy(x, nest_out.at[0], sem.at[0]),
-        pltpu.make_async_copy(p, parent_out, sem.at[1]),
-    ]
+def write_out(pieces, x, p, nest_out, parent_out, sem):
+    size = x.shape[0] // pieces
+    copies = [pltpu.make_async_copy(p, parent_out, sem.at[pieces])]
+    for c in range(pieces):
+        at = pl.ds(c * size, size)
+        copies.append(pltpu.make_async_copy(x.at[at], nest_out.at[0, at], sem.at[c]))
     for copy in copies:
         copy.start()
     for copy in copies:
@@ -480,7 +528,7 @@
             pltpu.VMEM((rows + 2, channels, width), bf16),
             pltpu.VMEM((rows + 2, channels, width), bf16),
             pltpu.VMEM((rows + 2, channels, 2 * LANES), bf16),
-            pltpu.VMEM((rows, channels, 2 * LANES), f32),
+            pltpu.VMEM((rows, channels, 2 * LANES), bf16),
             pltpu.VMEM((3 * groups, channels, cells), bf16),
             pltpu.VMEM((channels, channels), bf16),
             pltpu.VMEM((slots, cells, width), bf16),
@@ -488,6 +536,7 @@
             pltpu.VMEM((rows, width), jnp.int32),
             pltpu.VMEM((2, rows, width), f32),
             pltpu.VMEM((channels, width), bf16),
+            pltpu.VMEM((LANES // (2 * BW), LANES, 2 * LANES), bf16),
             pltpu.VMEM((2, channels * 2 * BW // LANES, LANES), bf16),
             pltpu.VMEM((2, channels * 2 * BW // LANES, LANES), bf16),
             pltpu.VMEM((width, LANES), bf16),
@@ -501,8 +550,8 @@
             pltpu.VMEM((parts, 2, part, cells), bf16),
             pltpu.VMEM((parts, part, cells), f32),
             pltpu.SemaphoreType.DMA((parts + 4 + slots,)),
-            pltpu.SemaphoreType.DMA((9,)),
-            pltpu.SemaphoreType.DMA((9,)),
+            pltpu.SemaphoreType.DMA((11,)),
+            pltpu.SemaphoreType.DMA((11,)),
             pltpu.SemaphoreType.DMA((4 * parts,)),
             pltpu.SemaphoreType.DMA((4 * parts,)),
             pltpu.SemaphoreType.DMA((2,)),
@@ -515,14 +564,15 @@
         ),
     )(intersection, nest_state, parent_state, mix_weight, interp_weight, avg_weight, land_mask)
     return pl.pallas_call(
-        write_out,
+        functools.partial(write_out, 8),
         out_shape=(
             jax.ShapeDtypeStruct(nest_state.shape, bf16),
             jax.ShapeDtypeStruct(parent_state.shape, bf16),
         ),
-        in_specs=[vmem, vmem],
+        in_specs=[hbm, hbm],
         out_specs=(hbm, hbm),
-        scratch_shapes=[pltpu.SemaphoreType.DMA((2,))],
+        scratch_shapes=[pltpu.SemaphoreType.DMA((9,))],
+        compiler_params=pltpu.CompilerParams(vmem_limit_bytes=8 * 2**20),
     )(x_new, p_new)
 
 

time: 71 us -> 54.6 us (0.77)
  the two profiles are of different devices: /device:TPU:32 before, /device:TPU:1 now
where the time goes in v3:
time: 54.6 us; the launch traced here: 53.6 us
  Pallas kernels  52.9 us (97%)
  between operations  0.64 us (1%)
    pallas_call x1, Pallas kernels, shards(): pl.pallas_call(functools.partial(kernel, groups, tiles, parts), out_shape...  50.1 us
    pallas_call x1, Pallas kernels, shards(): pl.pallas_call(functools.partial(write_out, 8), out_shape=(jax.ShapeDtype...  2.78 us

profile of v3, /device:TPU:1, one launch (start us, length us, event | category | flops | bytes accessed | tf_op | source)
XLA Modules:
  0.0 53.6 jit_solution(17285187175433160056)
XLA Ops:
  0.6 50.1 %shard_map.86 = (bf16[384,16,512]{2,1,0:T(8,128)(2,1)S(1)}, bf16[384,128]{1,0:T(8,128)(2,1)S(1)}) custom-call(s32[1,1,4]{2,1,0:T(1,128)} %picks.1, bf16[1,384,16,512]{3,2,1,0:T(8,128)(2,1)} %nest.1, bf16[384,128]{1,0:T(8,128)(2,1)} %parent.1, bf16[384,384]{1,0:T(8,128)(2,1)} %mix.1, bf16[1,1,4,128,512]{4,3,2,1,0:T(8,128)(2,1)} %interp.1, ...), custom_call_target="tpu_custom_call" | custom-call | tf_op jit(solution)/shard_map/pallas_call | solution.py:522
  50.8 2.8 %shard_map.87 = (bf16[1,384,16,512]{3,2,1,0:T(8,128)(2,1)}, bf16[384,128]{1,0:T(8,128)(2,1)}) custom-call(bf16[384,16,512]{2,1,0:T(8,128)(2,1)S(1)} %get-tuple-element.4.x, bf16[384,128]{1,0:T(8,128)(2,1)S(1)} %get-tuple-element.5.p), custom_call_target="tpu_custom_call" | custom-call | tf_op jit(solution)/shard_map/pallas_call | solution.py:566

commit v4 on v3

--- a/solution.py
+++ b/solution.py
@@ -9,6 +9,7 @@
 
 BW = 16
 LANES = 128
+SIDE = 4
 MESH = pl.DeviceIdType.MESH
 f32, bf16 = jnp.float32, jnp.bfloat16
 
@@ -71,7 +72,15 @@
         load.start()
     for load in (mix_load, land_load, w_load, *av_loads):
         load.start()
-    own_load.wait()
+    def rows_first(c):
+        x_loads[c].wait()
+
+        def body(i, carry):
+            at = pl.ds(pl.multiple_of(c * part + i * 16, 16), 16)
+            xa[1 : rows + 1, at, :] = jnp.swapaxes(x_out[at], 0, 1)
+            return carry
+
+        lax.fori_loop(0, part // 16, body, 0)
 
     @pl.when(first)
     def _():
@@ -89,6 +98,7 @@
         greet(to_up)
         greet((deep, up))
 
+    own_load.wait()
     own = cand.at[3 * n + 1]
     tile_up = remote(own, cand.at[3 * n], p_send.at[0], p_recv.at[0], to_up)
     tile_down = remote(own, cand.at[3 * n + 2], p_send.at[1], p_recv.at[1], to_down)
@@ -104,9 +114,12 @@
 
     over_up = remote(own, cand.at[3 * n], p_send.at[9], p_recv.at[9], (deep, up))
     over_down = remote(own, cand.at[3 * n + 2], p_send.at[9], p_recv.at[9], (deep, down))
-    deep_own = cand.at[3 * deep + 1]
-    beside_down = remote(deep_own, cand.at[3 * deep + 2], p_send.at[10], p_recv.at[10], to_down)
-    beside_up = remote(deep_own, cand.at[3 * deep], p_send.at[10], p_recv.at[10], to_up)
+    def beside(k, source, target, device):
+        return remote(cand.at[3 * deep + source], cand.at[3 * deep + target], p_send.at[10 + k], p_recv.at[10 + k], device)
+
+    beside_down = beside(0, 1, 2, to_down), beside(1, 0, 1, to_down)
+    beside_up = beside(0, 1, 0, to_up), beside(1, 2, 1, to_up)
+    after_first, before_last = t == 1, t == tiles - 2
 
     def pass_on(o):
         group_copies[o][0].start()
@@ -124,8 +137,7 @@
         tile_up.start()
         pl.when(t > 0)(tile_down.start)
         pl.when(last)(over_up.start)
-        for copy in group_copies[1]:
-            copy.start()
+        pass_on(1)
 
     def halos(state, step, c):
         k = (step * parts + c) * 2
@@ -163,14 +175,7 @@
 
     with jax.named_scope("rows_first"):
         for c in range(parts):
-            x_loads[c].wait()
-
-            def rows_first(i, carry, c=c):
-                at = pl.ds(pl.multiple_of(c * part + i * 16, 16), 16)
-                xa[1 : rows + 1, at, :] = jnp.swapaxes(x_out[at], 0, 1)
-                return carry
-
-            lax.fori_loop(0, part // 16, rows_first, 0)
+            rows_first(c)
             halo_start(xa, 0, c)
 
     source = lax.broadcasted_iota(jnp.int32, (LANES, 2 * LANES), 0)
@@ -212,14 +217,22 @@
 
         lax.fori_loop(begin, end, body, 0)
 
+    row_start, row_end = lax.rem(t, SIDE) == 0, lax.rem(t, SIDE) == SIDE - 1
     with jax.named_scope("first_inner"):
-        first_rows(0, (rows - 2) // 2)
+        first_rows(0, 3)
     with jax.named_scope("tile_on"):
-        pl.when(t < tiles - 1)(from_above)
-        pl.when(t > 0)(from_below)
-        group_copies[1][1].wait_recv()
-        pl.when(t == 1)(beside_down.start)
-        pl.when(t == tiles - 2)(beside_up.start)
+        pl.when(after_first)(from_below)
+        pl.when(jnp.logical_not(row_end))(from_above)
+        pl.when(jnp.logical_not(jnp.logical_or(row_start, after_first)))(from_below)
+
+        @pl.when(jnp.logical_or(after_first, before_last))
+        def _():
+            group_copies[1][1].wait_recv()
+
+        pl.when(after_first)(beside_down[0].start)
+        pl.when(before_last)(beside_up[0].start)
+    with jax.named_scope("first_inner"):
+        first_rows(3, (rows - 2) // 2)
 
     mid, low, high = slice(LANES, width - LANES), slice(0, LANES), slice(width - LANES, width)
 
@@ -248,25 +261,60 @@
             xa[r + 1, at, low] = y[:, :LANES]
             xa[r + 1, at, high] = y[:, LANES:]
 
-    def pairs(one_row, begin, end):
+    def quads(one_row, begin, end):
         def body(i, carry):
-            one_row(2 * i, 0, channels)
-            one_row(2 * i + 1, 0, channels)
+            for j in range(4):
+                one_row(begin + 4 * i + j, 0, channels)
             return carry
 
-        lax.fori_loop(begin // 2, end // 2, body, 0)
-
-    stops = [2 + 2 * ((rows - 4) // 2 * c // parts) for c in range(parts + 1)]
+        lax.fori_loop(0, (end - begin) // 4, body, 0)
+
+    theirs = cand.at[pl.ds(3 * deep, 3)]
+    onward = remote(theirs, theirs, p_send.at[8], p_recv.at[8], to_core)
+
+    stops = (2, 6, rows - 2)
     for c in range(parts):
+        if c == parts - 1:
+            with jax.named_scope("deep_tiles_wait"):
+
+                @pl.when(inside)
+                def _():
+                    pl.when(jnp.logical_not(after_first))(group_copies[0][1].wait_recv)
+                    pl.when(jnp.logical_not(before_last))(group_copies[2][1].wait_recv)
+
+                    @pl.when(jnp.logical_not(jnp.logical_or(after_first, before_last)))
+                    def _():
+                        group_copies[1][1].wait_recv()
+
+                    onward.start()
+
         with jax.named_scope("first_halo_wait"):
             halo_arrived(xa, 0, c)
         with jax.named_scope("first_edges"):
             update(0, c * part, part)
             update(rows - 1, c * part, part)
+        if c == 0:
+            with jax.named_scope("tile_on"):
+
+                @pl.when(after_first)
+                def _():
+                    group_copies[0][1].wait_recv()
+                    beside_down[1].start()
+
+                @pl.when(before_last)
+                def _():
+                    group_copies[2][1].wait_recv()
+                    beside_up[1].start()
+
         if c < parts - 1:
             halo_start(xb, 1, c)
+        if c == 0:
+            with jax.named_scope("tile_on"):
+                pl.when(jnp.logical_and(row_end, t < tiles - 1))(from_above)
+                pl.when(jnp.logical_and(row_start, t > 0))(from_below)
+        if c < parts - 1:
             with jax.named_scope("second_middle"):
-                pairs(update_mid, stops[c], stops[c + 1])
+                quads(update_mid, stops[c], stops[c + 1])
         if c == 1:
 
             @pl.when(first)
@@ -279,31 +327,25 @@
         pl.when(first)(from_below)
         pl.when(last)(from_above)
     with jax.named_scope("second_middle"):
-        pairs(update_mid, stops[parts - 1], stops[parts])
         update_mid(1, 0, channels)
         update_mid(rows - 2, 0, channels)
 
     w_load.wait()
     with jax.named_scope("deep_tiles_wait"):
-
-        @pl.when(inside)
-        def _():
-            group_copies[0][1].wait_recv()
-            group_copies[2][1].wait_recv()
 
         @pl.when(first)
         def _():
             over_up.wait_recv()
-            beside_down.wait_recv()
+            beside_down[0].wait_recv()
+            beside_down[1].wait_recv()
 
         @pl.when(last)
         def _():
             over_down.wait_recv()
-            beside_up.wait_recv()
-
-    theirs = cand.at[pl.ds(3 * deep, 3)]
-    onward = remote(theirs, theirs, p_send.at[8], p_recv.at[8], to_core)
-    onward.start()
+            beside_up[0].wait_recv()
+            beside_up[1].wait_recv()
+
+        pl.when(ends)(onward.start)
     with jax.named_scope("core_tiles_wait"):
         for o in range(3):
             group_copies[o][0].wait_recv()
@@ -336,21 +378,22 @@
         xf[row, at, :LANES] = (xb[row, at, low].astype(f32) + wide[:, :LANES]).astype(bf16)
         xf[row, at, LANES:] = (xb[row, at, high].astype(f32) + wide[:, LANES:]).astype(bf16)
 
-    def spread(b, carry):
-        value = strip_v[:, pl.ds(pl.multiple_of(b * LANES, LANES), LANES)]
-        for j in range(per):
-            wide = placed(value, j)
-            ws[per * b + j] = wide.astype(bf16)
-            fixed(per * b + j + 1, slice(0, channels), wide)
+    def spread(j, carry):
+        value = jnp.concatenate([strip_v[:, b * LANES : (b + 1) * LANES] for b in range(rows // per)], axis=0)
+        wide = placed(value, j)
+        for b in range(rows // per):
+            block = wide[b * channels : (b + 1) * channels]
+            ws[per * b + j] = block.astype(bf16)
+            fixed(per * b + j + 1, slice(0, channels), block)
         return carry
 
     with jax.named_scope("strip_spread"):
-        lax.fori_loop(0, rows // per, spread, 0)
+        lax.fori_loop(0, per, spread, 0)
 
     with jax.named_scope("second_outer"):
         update_out(1, 0, channels)
         update_out(rows - 2, 0, channels)
-        pairs(update_out, 2, rows - 2)
+        quads(update_out, 2, rows - 2)
 
     for load in av_loads:
         load.wait()
@@ -380,36 +423,37 @@
             remote(fbs.at[c, core_deep], r1.at[c, 1], f_send.at[5 * c + 1], f_recv.at[5 * c + 1], to_core),
         )
 
-    def deep_copy(c):
-        return remote(s2.at[c], r2.at[c], f_send.at[5 * c + 2], f_recv.at[5 * c + 2], to_deep)
-
     def tile_copies(c):
         return (
-            remote(s3.at[c, 0], r3.at[c, 0], f_send.at[5 * c + 3], f_recv.at[5 * c + 3], to_down),
-            remote(s3.at[c, 1], r3.at[c, 1], f_send.at[5 * c + 4], f_recv.at[5 * c + 4], to_up),
+            remote(s2.at[c, 0], r2.at[c, 0], f_send.at[5 * c + 2], f_recv.at[5 * c + 2], to_down),
+            remote(s2.at[c, 1], r2.at[c, 1], f_send.at[5 * c + 3], f_recv.at[5 * c + 3], to_up),
         )
+
+    def deep_copy(c):
+        return remote(s3.at[c], r3.at[c], f_send.at[5 * c + 4], f_recv.at[5 * c + 4], to_deep)
 
     def stage_core(c):
         for copy in core_copies(c):
             copy.wait_recv()
-        s2[c] = (fbs[c, deep].astype(f32) + r1[c, 1].astype(f32)).astype(bf16)
-        deep_copy(c).start()
-
-    def stage_deep(c):
-        deep_copy(c).wait_recv()
-        total = fbs[c, n].astype(f32) + r1[c, 0].astype(f32) + r2[c].astype(f32)
-        s3[c, 0] = total[0].astype(bf16)
-        s3[c, 1] = total[2].astype(bf16)
-        g1[c] = total[1]
+        for k, group in enumerate((n, deep)):
+            total = fbs[c, group].astype(f32) + r1[c, k].astype(f32)
+            s2[c, 0, k] = total[0].astype(bf16)
+            s2[c, 1, k] = total[2].astype(bf16)
+            g1[c, k] = total[1]
         for copy in tile_copies(c):
             copy.start()
 
     def stage_tile(c):
         for copy in tile_copies(c):
             copy.wait_recv()
+        s3[c] = (g1[c, 1] + r2[c, 0, 1].astype(f32) + r2[c, 1, 1].astype(f32)).astype(bf16)
+        deep_copy(c).start()
+        g1[c, 0] = g1[c, 0] + r2[c, 0, 0].astype(f32) + r2[c, 1, 0].astype(f32)
+
+    def stage_deep(c):
+        deep_copy(c).wait_recv()
         mine = cand[3 * n + 1, span(c), :].astype(f32)
-        total = mine + (g1[c] + r3[c, 0].astype(f32) + r3[c, 1].astype(f32))
-        p_out[span(c), :] = total.astype(bf16)
+        p_out[span(c), :] = (mine + (g1[c, 0] + r3[c].astype(f32))).astype(bf16)
 
     def channels_first(c):
         def body(i, carry):
@@ -455,37 +499,35 @@
                 fbs[c, slot // 3, slot % 3] = total.astype(bf16)
             for copy in core_copies(c):
                 copy.start()
-        if c > 0:
-            with jax.named_scope("feedback_core"):
-                stage_core(c - 1)
-    with jax.named_scope("channels_first"):
-        channels_first(0)
-    with jax.named_scope("feedback_core"):
-        stage_core(parts - 1)
-    with jax.named_scope("channels_first"):
-        for c in range(1, parts):
+    for c in range(parts):
+        with jax.named_scope("feedback_core"):
+            stage_core(c)
+        with jax.named_scope("channels_first"):
             channels_first(c)
+    for c in range(parts):
+        with jax.named_scope("feedback_tile"):
+            stage_tile(c)
     for c in range(parts):
         with jax.named_scope("feedback_deep"):
             stage_deep(c)
-    for c in range(parts):
-        with jax.named_scope("feedback_tile"):
-            stage_tile(c)
 
     with jax.named_scope("sent"):
         tile_up.wait_send()
         tile_down.wait_send()
         for copy, _ in group_copies:
             copy.wait_send()
-        group_copies[1][1].wait_send()
 
         @pl.when(inside)
         def _():
-            group_copies[0][1].wait_send()
-            group_copies[2][1].wait_send()
+            for _, copy in group_copies:
+                copy.wait_send()
 
         pl.when(ends)(over_up.wait_send)
-        pl.when(jnp.logical_or(t == 1, t == tiles - 2))(beside_up.wait_send)
+
+        @pl.when(jnp.logical_or(after_first, before_last))
+        def _():
+            for copy in beside_up:
+                copy.wait_send()
         onward.wait_send()
         pl.when(t < tiles - 1)(ring_up.wait_send)
         pl.when(t > 0)(ring_down.wait_send)
@@ -544,14 +586,14 @@
             pltpu.VMEM((channels, slots * cells), f32),
             pltpu.VMEM((parts, groups, 3, part, cells), bf16),
             pltpu.VMEM((parts, 2, 3, part, cells), bf16),
-            pltpu.VMEM((parts, 3, part, cells), bf16),
-            pltpu.VMEM((parts, 3, part, cells), bf16),
-            pltpu.VMEM((parts, 2, part, cells), bf16),
-            pltpu.VMEM((parts, 2, part, cells), bf16),
-            pltpu.VMEM((parts, part, cells), f32),
+            pltpu.VMEM((parts, 2, 2, part, cells), bf16),
+            pltpu.VMEM((parts, 2, 2, part, cells), bf16),
+            pltpu.VMEM((parts, part, cells), bf16),
+            pltpu.VMEM((parts, part, cells), bf16),
+            pltpu.VMEM((parts, 2, part, cells), f32),
             pltpu.SemaphoreType.DMA((parts + 4 + slots,)),
-            pltpu.SemaphoreType.DMA((11,)),
-            pltpu.SemaphoreType.DMA((11,)),
+            pltpu.SemaphoreType.DMA((12,)),
+            pltpu.SemaphoreType.DMA((12,)),
             pltpu.SemaphoreType.DMA((4 * parts,)),
             pltpu.SemaphoreType.DMA((4 * parts,)),
             pltpu.SemaphoreType.DMA((2,)),

time: 54.6 us -> 51.2 us (0.938); the launches traced: 53.6 us -> 51.1 us
  Pallas kernels: 52.9 us -> 50.5 us
    pallas_call x1, Pallas kernels: 50.1 us -> 47.7 us  [shards(): pl.pallas_call(functools.partial(kernel, groups, tiles, parts), out_shape...]
where the time goes in v4:
time: 51.2 us; the launch traced here: 51.1 us
  Pallas kernels  50.5 us (99%)
  between operations  0.64 us (1%)
    pallas_call x1, Pallas kernels, shards(): pl.pallas_call(functools.partial(kernel, groups, tiles, parts), out_shape...  47.7 us
    pallas_call x1, Pallas kernels, shards(): pl.pallas_call(functools.partial(write_out, 8), out_shape=(jax.ShapeDtype...  2.78 us

profile of v4, /device:TPU:1, one launch (start us, length us, event | category | flops | bytes accessed | tf_op | source)
XLA Modules:
  0.0 51.1 jit_solution(2366781387063604265)
XLA Ops:
  0.6 47.7 %shard_map.86 = (bf16[384,16,512]{2,1,0:T(8,128)(2,1)S(1)}, bf16[384,128]{1,0:T(8,128)(2,1)S(1)}) custom-call(s32[1,1,4]{2,1,0:T(1,128)} %picks.1, bf16[1,384,16,512]{3,2,1,0:T(8,128)(2,1)} %nest.1, bf16[384,128]{1,0:T(8,128)(2,1)} %parent.1, bf16[384,384]{1,0:T(8,128)(2,1)} %mix.1, bf16[1,1,4,128,512]{4,3,2,1,0:T(8,128)(2,1)} %interp.1, ...), custom_call_target="tpu_custom_call" | custom-call | tf_op jit(solution)/shard_map/pallas_call | solution.py:564
  48.3 2.8 %shard_map.87 = (bf16[1,384,16,512]{3,2,1,0:T(8,128)(2,1)}, bf16[384,128]{1,0:T(8,128)(2,1)}) custom-call(bf16[384,16,512]{2,1,0:T(8,128)(2,1)S(1)} %get-tuple-element.4.x, bf16[384,128]{1,0:T(8,128)(2,1)S(1)} %get-tuple-element.5.p), custom_call_target="tpu_custom_call" | custom-call | tf_op jit(solution)/shard_map/pallas_call | solution.py:608

commit v5 on v4

--- a/solution.py
+++ b/solution.py
@@ -23,8 +23,8 @@
     groups, tiles, parts,
     picks, nest, parent, mix, interp, avg, land,
     x_out, p_out,
-    xa, xb, xf, ws, cand, m_v, w_v, av_v, land_v, coef, strip_v, place_v, pack_v, ring_v, pool_v, tops, fb, fbs, r1, s2, r2, s3, r3, g1,
-    load_sem, p_send, p_recv, h_send, h_recv, s_send, s_recv, f_send, f_recv,
+    xa, xb, xf, ws, cand, hub_v, m_v, w_v, av_v, land_v, coef, strip_v, place_v, pack_v, ring_v, pool_v, tops, fb, fbs, r1, s2, r2, s3, r3, g1,
+    load_sem, p_send, p_recv, d_send, d_recv, h_send, h_recv, s_send, s_recv, f_send, f_recv,
 ):
     channels, rows, width = x_out.shape
     part = channels // parts
@@ -39,6 +39,8 @@
     first, last = t == 0, t == tiles - 1
     inside = jnp.logical_and(t > 0, t < tiles - 1)
     ends = jnp.logical_or(first, last)
+    hub_tile = tiles // 2 + SIDE - 1
+    hub = t == hub_tile
 
     def remote(src, dst, send, recv, device):
         return pltpu.make_async_remote_copy(
@@ -92,11 +94,18 @@
     def _():
         pl.semaphore_wait(barrier, 4)
 
+    @pl.when(hub)
+    def _():
+        greet((n, tiles - 1))
+        greet((deep, tiles - 1))
+
     @pl.when(last)
     def _():
-        pl.semaphore_wait(barrier, 5)
+        pl.semaphore_wait(barrier, 7)
         greet(to_up)
         greet((deep, up))
+        greet((n, hub_tile))
+        greet((deep, hub_tile))
 
     own_load.wait()
     own = cand.at[3 * n + 1]
@@ -118,8 +127,18 @@
         return remote(cand.at[3 * deep + source], cand.at[3 * deep + target], p_send.at[10 + k], p_recv.at[10 + k], device)
 
     beside_down = beside(0, 1, 2, to_down), beside(1, 0, 1, to_down)
-    beside_up = beside(0, 1, 0, to_up), beside(1, 2, 1, to_up)
-    after_first, before_last = t == 1, t == tiles - 2
+    after_first = t == 1
+    to_hub = [
+        remote(cand.at[3 * n + 1 - k], hub_v.at[k], d_send.at[k], d_recv.at[k], (deep, hub_tile)) for k in range(2)
+    ]
+    from_hub = [
+        remote(hub_v.at[k], cand.at[3 * deep + 1 - k], d_send.at[2 + k], d_recv.at[2 + k], (n, tiles - 1))
+        for k in range(2)
+    ]
+
+    def hub_pass(k):
+        to_hub[k].wait_recv()
+        from_hub[k].start()
 
     def pass_on(o):
         group_copies[o][0].start()
@@ -134,23 +153,35 @@
         pass_on(2)
 
     with jax.named_scope("own_tile"):
+        pl.when(last)(to_hub[0].start)
         tile_up.start()
         pl.when(t > 0)(tile_down.start)
-        pl.when(last)(over_up.start)
         pass_on(1)
 
+    def halo_up(state, step, c):
+        k = (step * parts + c) * 2
+        return remote(state.at[rows, span(c)], state.at[0, span(c)], h_send.at[k], h_recv.at[k], to_up)
+
+    def halo_down(state, step, c):
+        k = (step * parts + c) * 2 + 1
+        return remote(state.at[1, span(c)], state.at[rows + 1, span(c)], h_send.at[k], h_recv.at[k], to_down)
+
     def halos(state, step, c):
-        k = (step * parts + c) * 2
-        return (
-            remote(state.at[rows, span(c)], state.at[0, span(c)], h_send.at[k], h_recv.at[k], to_up),
-            remote(state.at[1, span(c)], state.at[rows + 1, span(c)], h_send.at[k + 1], h_recv.at[k + 1], to_down),
-        )
+        return halo_up(state, step, c), halo_down(state, step, c)
 
     def halo_start(state, step, c):
         upward, downward = halos(state, step, c)
         pl.when(t < tiles - 1)(upward.start)
         pl.when(t > 0)(downward.start)
 
+    def halo_one_way(state, step, c):
+        upward, downward = halos(state, step, c)
+        pl.when(t < tiles - 1)(upward.start)
+        pl.when(t > 1)(downward.start)
+
+    def halo_held(state, step, c):
+        pl.when(after_first)(halo_down(state, step, c).start)
+
     def halo_arrived(state, step, c):
         upward, downward = halos(state, step, c)
         pl.when(t > 0)(upward.wait_recv)
@@ -176,7 +207,7 @@
     with jax.named_scope("rows_first"):
         for c in range(parts):
             rows_first(c)
-            halo_start(xa, 0, c)
+            (halo_start if c < parts - 1 else halo_one_way)(xa, 0, c)
 
     source = lax.broadcasted_iota(jnp.int32, (LANES, 2 * LANES), 0)
     target = lax.broadcasted_iota(jnp.int32, (LANES, 2 * LANES), 1)
@@ -218,6 +249,9 @@
         lax.fori_loop(begin, end, body, 0)
 
     row_start, row_end = lax.rem(t, SIDE) == 0, lax.rem(t, SIDE) == SIDE - 1
+    beside_row = jnp.logical_or(row_start, row_end)
+    far = jnp.logical_or(t == tiles // 2 - 1, t == tiles // 2)
+    strip_early = jnp.logical_or(ends, far)
     with jax.named_scope("first_inner"):
         first_rows(0, 3)
     with jax.named_scope("tile_on"):
@@ -225,12 +259,17 @@
         pl.when(jnp.logical_not(row_end))(from_above)
         pl.when(jnp.logical_not(jnp.logical_or(row_start, after_first)))(from_below)
 
-        @pl.when(jnp.logical_or(after_first, before_last))
+
+        @pl.when(last)
+        def _():
+            to_hub[1].start()
+            over_up.start()
+
+        @pl.when(after_first)
         def _():
             group_copies[1][1].wait_recv()
-
-        pl.when(after_first)(beside_down[0].start)
-        pl.when(before_last)(beside_up[0].start)
+            beside_down[0].start()
+
     with jax.named_scope("first_inner"):
         first_rows(3, (rows - 2) // 2)
 
@@ -261,139 +300,193 @@
             xa[r + 1, at, low] = y[:, :LANES]
             xa[r + 1, at, high] = y[:, LANES:]
 
-    def quads(one_row, begin, end):
+    def quads(one_row, row, begin, end, start, count):
         def body(i, carry):
             for j in range(4):
-                one_row(begin + 4 * i + j, 0, channels)
+                one_row(row + 4 * i + j, start, count)
             return carry
 
-        lax.fori_loop(0, (end - begin) // 4, body, 0)
-
-    theirs = cand.at[pl.ds(3 * deep, 3)]
-    onward = remote(theirs, theirs, p_send.at[8], p_recv.at[8], to_core)
-
-    stops = (2, 6, rows - 2)
-    for c in range(parts):
-        if c == parts - 1:
-            with jax.named_scope("deep_tiles_wait"):
-
-                @pl.when(inside)
-                def _():
-                    pl.when(jnp.logical_not(after_first))(group_copies[0][1].wait_recv)
-                    pl.when(jnp.logical_not(before_last))(group_copies[2][1].wait_recv)
-
-                    @pl.when(jnp.logical_not(jnp.logical_or(after_first, before_last)))
-                    def _():
-                        group_copies[1][1].wait_recv()
-
-                    onward.start()
-
+        lax.fori_loop(begin, end, body, 0)
+
+    onward = [
+        remote(cand.at[3 * deep + o], cand.at[3 * deep + o], d_send.at[4 + o], d_recv.at[4 + o], to_core) for o in range(3)
+    ]
+
+    def deep_tiles():
+        @pl.when(jnp.logical_not(after_first))
+        def _():
+            group_copies[1][1].wait_recv()
+            group_copies[0][1].wait_recv()
+
+        onward[1].start()
+        onward[0].start()
+        group_copies[2][1].wait_recv()
+        onward[2].start()
+
+    def middle_quads(begin, end):
+        with jax.named_scope("second_middle"):
+            quads(update_mid, 2, begin, end, 0, channels)
+
+    early = jnp.where(beside_row, 1, 0)
+    sooner = jnp.where(far, 3, early)
+    later = jnp.where(far, 3, early + 1)
+
+    def first_edges(c):
         with jax.named_scope("first_halo_wait"):
             halo_arrived(xa, 0, c)
         with jax.named_scope("first_edges"):
             update(0, c * part, part)
             update(rows - 1, c * part, part)
-        if c == 0:
-            with jax.named_scope("tile_on"):
-
-                @pl.when(after_first)
-                def _():
-                    group_copies[0][1].wait_recv()
-                    beside_down[1].start()
-
-                @pl.when(before_last)
-                def _():
-                    group_copies[2][1].wait_recv()
-                    beside_up[1].start()
-
-        if c < parts - 1:
-            halo_start(xb, 1, c)
-        if c == 0:
-            with jax.named_scope("tile_on"):
-                pl.when(jnp.logical_and(row_end, t < tiles - 1))(from_above)
-                pl.when(jnp.logical_and(row_start, t > 0))(from_below)
-        if c < parts - 1:
-            with jax.named_scope("second_middle"):
-                quads(update_mid, stops[c], stops[c + 1])
-        if c == 1:
-
-            @pl.when(first)
-            def _():
-                pl.semaphore_wait(barrier, 2)
-                tile_down.start()
-                over_down.start()
-
+
+    middle_quads(0, early)
+    with jax.named_scope("tile_on"):
+        pl.when(jnp.logical_and(row_end, t < tiles - 1))(from_above)
+        pl.when(jnp.logical_and(row_start, t > 0))(from_below)
+
+        @pl.when(hub)
+        def _():
+            pl.semaphore_wait(barrier, 2)
+            hub_pass(0)
+
+        @pl.when(first)
+        def _():
+            pl.semaphore_wait(barrier, 2)
+            tile_down.start()
+            over_down.start()
+
+    middle_quads(early, sooner)
+    first_edges(0)
+    with jax.named_scope("tile_on"):
+
+        @pl.when(after_first)
+        def _():
+            group_copies[0][1].wait_recv()
+            beside_down[1].start()
+
+        halo_held(xa, 0, parts - 1)
+
+    halo_start(xb, 1, 0)
+    middle_quads(sooner, later)
+    with jax.named_scope("deep_tiles_wait"):
+        pl.when(hub)(lambda: hub_pass(1))
+        pl.when(jnp.logical_and(inside, beside_row))(deep_tiles)
+    first_edges(1)
+    middle_quads(later, 2)
+    with jax.named_scope("deep_tiles_wait"):
+        pl.when(jnp.logical_not(beside_row))(deep_tiles)
+    middle_quads(jnp.maximum(later, 2), 3)
     with jax.named_scope("tile_on"):
         pl.when(first)(from_below)
         pl.when(last)(from_above)
+
+    cells = 2 * BW
+    per = LANES // cells
+    short = channels // per
+
+    def pack(begin):
+        return jnp.concatenate([strip_v[q * short : (q + 1) * short, begin : begin + cells] for q in range(per)], axis=1)
+
+    ring_up = remote(pack_v.at[0], ring_v.at[0], s_send.at[0], s_recv.at[0], to_up)
+    ring_down = remote(pack_v.at[1], ring_v.at[1], s_send.at[1], s_recv.at[1], to_down)
+
+    def boundary_strip():
+        with jax.named_scope("deep_tiles_wait"):
+
+            @pl.when(first)
+            def _():
+                beside_down[0].wait_recv()
+                onward[2].start()
+                beside_down[1].wait_recv()
+                onward[1].start()
+                over_up.wait_recv()
+                onward[0].start()
+
+            @pl.when(last)
+            def _():
+                from_hub[0].wait_recv()
+                onward[1].start()
+                from_hub[1].wait_recv()
+                onward[0].start()
+                over_down.wait_recv()
+                onward[2].start()
+
+        with jax.named_scope("core_tiles_wait"):
+            for o in range(3):
+                group_copies[o][0].wait_recv()
+            for copy in onward:
+                copy.wait_recv()
+        with jax.named_scope("strip"):
+            picked = jnp.concatenate([cand[picks[0, 0, k]] for k in range(slots)], axis=1)
+            weights = w_v[...].reshape(slots * LANES, width)
+            strip_v[...] = jnp.dot(picked, weights, preferred_element_type=f32).astype(bf16)
+        with jax.named_scope("strip_send"):
+            pack_v[0] = pack(width - cells)
+            pack_v[1] = pack(0)
+            pl.when(t < tiles - 1)(ring_up.start)
+            pl.when(t > 0)(ring_down.start)
+            halo_start(xb, 1, 1)
+
+    def placed(value, j):
+        return jnp.dot(value, place_v[j], preferred_element_type=f32)
+
+    def fixed(row, at, wide):
+        xf[row, at, :LANES] = (xb[row, at, low].astype(f32) + wide[:, :LANES]).astype(bf16)
+        xf[row, at, LANES:] = (xb[row, at, high].astype(f32) + wide[:, LANES:]).astype(bf16)
+
+    everything = slice(0, channels)
+
+    def spread_strip():
+        def spread(j, carry):
+            value = jnp.concatenate([strip_v[:, b * LANES : (b + 1) * LANES] for b in range(rows // per)], axis=0)
+            wide = placed(value, j)
+            for b in range(rows // per):
+                block = wide[b * channels : (b + 1) * channels]
+                ws[per * b + j] = block.astype(bf16)
+                fixed(per * b + j + 1, everything, block)
+            return carry
+
+        with jax.named_scope("strip_spread"):
+            lax.fori_loop(0, per, spread, 0)
+
+    most = channels - part
+
+    def outer_quads(start, count):
+        with jax.named_scope("second_outer"):
+            quads(update_out, 2, 0, (rows - 4) // 4, start, count)
+
+    def outer_near(start, count):
+        with jax.named_scope("second_outer"):
+            update_out(1, start, count)
+            update_out(rows - 2, start, count)
+
+    w_load.wait()
+
+    pl.when(strip_early)(boundary_strip)
+
+    @pl.when(ends)
+    def _():
+        spread_strip()
+        outer_quads(0, most)
+
+    first_edges(parts - 1)
     with jax.named_scope("second_middle"):
         update_mid(1, 0, channels)
         update_mid(rows - 2, 0, channels)
-
-    w_load.wait()
-    with jax.named_scope("deep_tiles_wait"):
-
-        @pl.when(first)
-        def _():
-            over_up.wait_recv()
-            beside_down[0].wait_recv()
-            beside_down[1].wait_recv()
-
-        @pl.when(last)
-        def _():
-            over_down.wait_recv()
-            beside_up[0].wait_recv()
-            beside_up[1].wait_recv()
-
-        pl.when(ends)(onward.start)
-    with jax.named_scope("core_tiles_wait"):
-        for o in range(3):
-            group_copies[o][0].wait_recv()
-        onward.wait_recv()
-    with jax.named_scope("strip"):
-        picked = jnp.concatenate([cand[picks[0, 0, k]] for k in range(slots)], axis=1)
-        weights = w_v[...].reshape(slots * LANES, width)
-        strip_v[...] = jnp.dot(picked, weights, preferred_element_type=f32).astype(bf16)
-
-    cells = 2 * BW
-    per = LANES // cells
-    short = channels // per
-
-    def pack(begin):
-        return jnp.concatenate([strip_v[q * short : (q + 1) * short, begin : begin + cells] for q in range(per)], axis=1)
-
-    ring_up = remote(pack_v.at[0], ring_v.at[0], s_send.at[0], s_recv.at[0], to_up)
-    ring_down = remote(pack_v.at[1], ring_v.at[1], s_send.at[1], s_recv.at[1], to_down)
-    with jax.named_scope("strip_send"):
-        pack_v[0] = pack(width - cells)
-        pack_v[1] = pack(0)
-        pl.when(t < tiles - 1)(ring_up.start)
-        pl.when(t > 0)(ring_down.start)
-        halo_start(xb, 1, parts - 1)
-
-    def placed(value, j):
-        return jnp.dot(value, place_v[j], preferred_element_type=f32)
-
-    def fixed(row, at, wide):
-        xf[row, at, :LANES] = (xb[row, at, low].astype(f32) + wide[:, :LANES]).astype(bf16)
-        xf[row, at, LANES:] = (xb[row, at, high].astype(f32) + wide[:, LANES:]).astype(bf16)
-
-    def spread(j, carry):
-        value = jnp.concatenate([strip_v[:, b * LANES : (b + 1) * LANES] for b in range(rows // per)], axis=0)
-        wide = placed(value, j)
-        for b in range(rows // per):
-            block = wide[b * channels : (b + 1) * channels]
-            ws[per * b + j] = block.astype(bf16)
-            fixed(per * b + j + 1, slice(0, channels), block)
-        return carry
-
-    with jax.named_scope("strip_spread"):
-        lax.fori_loop(0, per, spread, 0)
-
-    with jax.named_scope("second_outer"):
-        update_out(1, 0, channels)
-        update_out(rows - 2, 0, channels)
-        quads(update_out, 2, rows - 2)
+    pl.when(jnp.logical_not(strip_early))(boundary_strip)
+    halo_start(xb, 1, parts - 1)
+
+    @pl.when(ends)
+    def _():
+        with jax.named_scope("strip_spread"):
+            for r in (0, rows - 1):
+                fixed(r + 1, everything, ws[r].astype(f32))
+
+    @pl.when(inside)
+    def _():
+        spread_strip()
+        outer_quads(0, most)
+
+    outer_near(0, most)
 
     for load in av_loads:
         load.wait()
@@ -410,12 +503,13 @@
     def averaged(total):
         return jnp.dot(total.astype(bf16), pool_v[...], preferred_element_type=f32).astype(bf16)
 
-    everything = slice(0, channels)
-    with jax.named_scope("feedback_inner"):
-        tops[0] = row_total(1, 3, everything)
-        tops[1] = row_total(rows - 4, 3, everything)
-        middle = jnp.concatenate([averaged(row_total(4 * b, 4, everything)) for b in range(1, bands - 1)], axis=1)
-        fb[...] = jnp.dot(middle, av_v[LANES : (bands - 1) * LANES, :], preferred_element_type=f32)
+    def feedback_inner(start, count):
+        with jax.named_scope("feedback_inner"):
+            at = slice(start, start + count)
+            tops[0, at] = row_total(1, 3, at)
+            tops[1, at] = row_total(rows - 4, 3, at)
+            middle = jnp.concatenate([averaged(row_total(4 * b, 4, at)) for b in range(1, bands - 1)], axis=1)
+            fb[at] = jnp.dot(middle, av_v[LANES : (bands - 1) * LANES, :], preferred_element_type=f32)
 
     def core_copies(c):
         return (
@@ -463,6 +557,8 @@
 
         lax.fori_loop(0, part // 16, body, 0)
 
+    feedback_inner(0, most)
+
     with jax.named_scope("strip_wait"):
         pl.when(t > 0)(ring_up.wait_recv)
         pl.when(t < tiles - 1)(ring_down.wait_recv)
@@ -478,6 +574,13 @@
     for c in range(parts):
         halo_sent(xa, 0, c)
     for c in range(parts):
+        if c == parts - 1:
+            outer_quads(c * part, part)
+            outer_near(c * part, part)
+            feedback_inner(c * part, part)
+            with jax.named_scope("feedback_core"):
+                for k in range(c):
+                    stage_core(k)
         with jax.named_scope("second_halo_wait"):
             halo_arrived(xb, 1, c)
         with jax.named_scope("second_edges"):
@@ -499,10 +602,12 @@
                 fbs[c, slot // 3, slot % 3] = total.astype(bf16)
             for copy in core_copies(c):
                 copy.start()
-    for c in range(parts):
-        with jax.named_scope("feedback_core"):
-            stage_core(c)
-        with jax.named_scope("channels_first"):
+    with jax.named_scope("channels_first"):
+        channels_first(0)
+    with jax.named_scope("feedback_core"):
+        stage_core(parts - 1)
+    with jax.named_scope("channels_first"):
+        for c in range(1, parts):
             channels_first(c)
     for c in range(parts):
         with jax.named_scope("feedback_tile"):
@@ -524,11 +629,22 @@
 
         pl.when(ends)(over_up.wait_send)
 
-        @pl.when(jnp.logical_or(after_first, before_last))
-        def _():
-            for copy in beside_up:
+        @pl.when(after_first)
+        def _():
+            for copy in beside_down:
                 copy.wait_send()
-        onward.wait_send()
+
+        @pl.when(last)
+        def _():
+            for copy in to_hub:
+                copy.wait_send()
+
+        @pl.when(hub)
+        def _():
+            for copy in from_hub:
+                copy.wait_send()
+        for copy in onward:
+            copy.wait_send()
         pl.when(t < tiles - 1)(ring_up.wait_send)
         pl.when(t > 0)(ring_down.wait_send)
         for c in range(parts):
@@ -572,6 +688,7 @@
             pltpu.VMEM((rows + 2, channels, 2 * LANES), bf16),
             pltpu.VMEM((rows, channels, 2 * LANES), bf16),
             pltpu.VMEM((3 * groups, channels, cells), bf16),
+            pltpu.VMEM((2, channels, cells), bf16),
             pltpu.VMEM((channels, channels), bf16),
             pltpu.VMEM((slots, cells, width), bf16),
             pltpu.VMEM((width, slots * cells), bf16),
@@ -594,6 +711,8 @@
             pltpu.SemaphoreType.DMA((parts + 4 + slots,)),
             pltpu.SemaphoreType.DMA((12,)),
             pltpu.SemaphoreType.DMA((12,)),
+            pltpu.SemaphoreType.DMA((7,)),
+            pltpu.SemaphoreType.DMA((7,)),
             pltpu.SemaphoreType.DMA((4 * parts,)),
             pltpu.SemaphoreType.DMA((4 * parts,)),
             pltpu.SemaphoreType.DMA((2,)),

time: 51.2 us -> 48.4 us (0.945); the launches traced: 51.1 us -> 47.8 us
  Pallas kernels: 50.5 us -> 47 us
    pallas_call x1, Pallas kernels: 47.7 us -> 44.2 us  [shards(): pl.pallas_call(functools.partial(kernel, groups, tiles, parts), out_shape...]
where the time goes in v5:
time: 48.4 us; the launch traced here: 47.8 us
  Pallas kernels  47 us (97%)
  between operations  0.8 us (2%)
    pallas_call x1, Pallas kernels, shards(): pl.pallas_call(functools.partial(kernel, groups, tiles, parts), out_shape...  44.2 us
    pallas_call x1, Pallas kernels, shards(): pl.pallas_call(functools.partial(write_out, 8), out_shape=(jax.ShapeDtype...  2.78 us

profile of v5, /device:TPU:1, one launch (start us, length us, event | category | flops | bytes accessed | tf_op | source)
XLA Modules:
  0.0 47.8 jit_solution(12829317794899538506)
XLA Ops:
  0.6 44.2 %shard_map.86 = (bf16[384,16,512]{2,1,0:T(8,128)(2,1)S(1)}, bf16[384,128]{1,0:T(8,128)(2,1)S(1)}) custom-call(s32[1,1,4]{2,1,0:T(1,128)} %picks.1, bf16[1,384,16,512]{3,2,1,0:T(8,128)(2,1)} %nest.1, bf16[384,128]{1,0:T(8,128)(2,1)} %parent.1, bf16[384,384]{1,0:T(8,128)(2,1)} %mix.1, bf16[1,1,4,128,512]{4,3,2,1,0:T(8,128)(2,1)} %interp.1, ...), custom_call_target="tpu_custom_call" | custom-call | tf_op jit(solution)/shard_map/pallas_call | solution.py:680
  44.8 2.8 %shard_map.87 = (bf16[1,384,16,512]{3,2,1,0:T(8,128)(2,1)}, bf16[384,128]{1,0:T(8,128)(2,1)}) custom-call(bf16[384,16,512]{2,1,0:T(8,128)(2,1)S(1)} %get-tuple-element.4.x, bf16[384,128]{1,0:T(8,128)(2,1)S(1)} %get-tuple-element.5.p), custom_call_target="tpu_custom_call" | custom-call | tf_op jit(solution)/shard_map/pallas_call | solution.py:727

commit v6 on v5

--- a/solution.py
+++ b/solution.py
@@ -39,6 +39,9 @@
     first, last = t == 0, t == tiles - 1
     inside = jnp.logical_and(t > 0, t < tiles - 1)
     ends = jnp.logical_or(first, last)
+    over_above = jnp.logical_or(t == tiles // 2 - 1, last)
+    over_below = jnp.logical_or(t == tiles // 2, first)
+    far = jnp.logical_or(t == tiles // 2 - 1, t == tiles // 2)
     hub_tile = tiles // 2 + SIDE - 1
     hub = t == hub_tile
 
@@ -56,6 +59,8 @@
     greet(to_deep)
     pl.when(t < tiles - 1)(lambda: greet(to_up))
     pl.when(t > 0)(lambda: greet(to_down))
+    pl.when(t == tiles // 2 - 1)(lambda: greet((deep, up)))
+    pl.when(t == tiles // 2)(lambda: greet((deep, down)))
 
     def span(c):
         return pl.ds(c * part, part)
@@ -90,9 +95,13 @@
         greet(to_down)
         greet((deep, down))
 
-    @pl.when(inside)
+    @pl.when(jnp.logical_and(inside, jnp.logical_not(far)))
     def _():
         pl.semaphore_wait(barrier, 4)
+
+    @pl.when(far)
+    def _():
+        pl.semaphore_wait(barrier, 5)
 
     @pl.when(hub)
     def _():
@@ -250,8 +259,7 @@
 
     row_start, row_end = lax.rem(t, SIDE) == 0, lax.rem(t, SIDE) == SIDE - 1
     beside_row = jnp.logical_or(row_start, row_end)
-    far = jnp.logical_or(t == tiles // 2 - 1, t == tiles // 2)
-    strip_early = jnp.logical_or(ends, far)
+    strip_early = jnp.logical_or(first, far)
     with jax.named_scope("first_inner"):
         first_rows(0, 3)
     with jax.named_scope("tile_on"):
@@ -463,7 +471,7 @@
 
     pl.when(strip_early)(boundary_strip)
 
-    @pl.when(ends)
+    @pl.when(first)
     def _():
         spread_strip()
         outer_quads(0, most)
@@ -475,13 +483,13 @@
     pl.when(jnp.logical_not(strip_early))(boundary_strip)
     halo_start(xb, 1, parts - 1)
 
-    @pl.when(ends)
+    @pl.when(first)
     def _():
         with jax.named_scope("strip_spread"):
             for r in (0, rows - 1):
                 fixed(r + 1, everything, ws[r].astype(f32))
 
-    @pl.when(inside)
+    @pl.when(t > 0)
     def _():
         spread_strip()
         outer_quads(0, most)
@@ -511,20 +519,26 @@
             middle = jnp.concatenate([averaged(row_total(4 * b, 4, at)) for b in range(1, bands - 1)], axis=1)
             fb[at] = jnp.dot(middle, av_v[LANES : (bands - 1) * LANES, :], preferred_element_type=f32)
 
+    up_group, down_group = jnp.where(over_above, deep, n), jnp.where(over_below, deep, n)
+
     def core_copies(c):
         return (
-            remote(fbs.at[c, core], r1.at[c, 0], f_send.at[5 * c], f_recv.at[5 * c], to_core),
-            remote(fbs.at[c, core_deep], r1.at[c, 1], f_send.at[5 * c + 1], f_recv.at[5 * c + 1], to_core),
+            remote(fbs.at[c, core], r1.at[c, 0], f_send.at[7 * c], f_recv.at[7 * c], to_core),
+            remote(fbs.at[c, core_deep], r1.at[c, 1], f_send.at[7 * c + 1], f_recv.at[7 * c + 1], to_core),
         )
 
-    def tile_copies(c):
-        return (
-            remote(s2.at[c, 0], r2.at[c, 0], f_send.at[5 * c + 2], f_recv.at[5 * c + 2], to_down),
-            remote(s2.at[c, 1], r2.at[c, 1], f_send.at[5 * c + 3], f_recv.at[5 * c + 3], to_up),
-        )
+    def tile_copy(c, way, k, device):
+        i = 7 * c + 2 + 2 * way + k
+        return remote(s2.at[c, way, k], r2.at[c, way, k], f_send.at[i], f_recv.at[i], device)
+
+    def down_copies(c):
+        return tile_copy(c, 0, 0, to_down), tile_copy(c, 0, 1, (down_group, down))
+
+    def up_copies(c):
+        return tile_copy(c, 1, 0, to_up), tile_copy(c, 1, 1, (up_group, up))
 
     def deep_copy(c):
-        return remote(s3.at[c], r3.at[c], f_send.at[5 * c + 4], f_recv.at[5 * c + 4], to_deep)
+        return remote(s3.at[c], r3.at[c], f_send.at[7 * c + 6], f_recv.at[7 * c + 6], to_deep)
 
     def stage_core(c):
         for copy in core_copies(c):
@@ -534,17 +548,38 @@
             s2[c, 0, k] = total[0].astype(bf16)
             s2[c, 1, k] = total[2].astype(bf16)
             g1[c, k] = total[1]
-        for copy in tile_copies(c):
+        for copy in (*down_copies(c), *up_copies(c)):
             copy.start()
 
     def stage_tile(c):
-        for copy in tile_copies(c):
-            copy.wait_recv()
-        s3[c] = (g1[c, 1] + r2[c, 0, 1].astype(f32) + r2[c, 1, 1].astype(f32)).astype(bf16)
+        @pl.when(jnp.logical_not(over_above))
+        def _():
+            for copy in down_copies(c):
+                copy.wait_recv()
+            g1[c] = g1[c] + r2[c, 0].astype(f32)
+
+        @pl.when(jnp.logical_not(over_below))
+        def _():
+            for copy in up_copies(c):
+                copy.wait_recv()
+            g1[c] = g1[c] + r2[c, 1].astype(f32)
+
+        s3[c] = g1[c, 1].astype(bf16)
         deep_copy(c).start()
-        g1[c, 0] = g1[c, 0] + r2[c, 0, 0].astype(f32) + r2[c, 1, 0].astype(f32)
 
     def stage_deep(c):
+        @pl.when(over_above)
+        def _():
+            for copy in down_copies(c):
+                copy.wait_recv()
+            g1[c, 0] = g1[c, 0] + r2[c, 0, 0].astype(f32) + r2[c, 0, 1].astype(f32)
+
+        @pl.when(over_below)
+        def _():
+            for copy in up_copies(c):
+                copy.wait_recv()
+            g1[c, 0] = g1[c, 0] + r2[c, 1, 0].astype(f32) + r2[c, 1, 1].astype(f32)
+
         deep_copy(c).wait_recv()
         mine = cand[3 * n + 1, span(c), :].astype(f32)
         p_out[span(c), :] = (mine + (g1[c, 0] + r3[c].astype(f32))).astype(bf16)
@@ -652,7 +687,7 @@
             for copy in core_copies(c):
                 copy.wait_send()
             deep_copy(c).wait_send()
-            for copy in tile_copies(c):
+            for copy in (*down_copies(c), *up_copies(c)):
                 copy.wait_send()
 
 
@@ -717,8 +752,8 @@
             pltpu.SemaphoreType.DMA((4 * parts,)),
             pltpu.SemaphoreType.DMA((2,)),
             pltpu.SemaphoreType.DMA((2,)),
-            pltpu.SemaphoreType.DMA((5 * parts,)),
-            pltpu.SemaphoreType.DMA((5 * parts,)),
+            pltpu.SemaphoreType.DMA((7 * parts,)),
+            pltpu.SemaphoreType.DMA((7 * parts,)),
         ],
         compiler_params=pltpu.CompilerParams(
             collective_id=0, has_side_effects=True, vmem_limit_bytes=48 * 2**20

time: 48.4 us -> 45.6 us (0.942)
  Pallas kernels: 47 us -> 44.6 us
    pallas_call x1, Pallas kernels: 44.2 us -> 41.9 us  [shards(): pl.pallas_call(functools.partial(kernel, groups, tiles, parts), out_shape...]
where the time goes in v6:
time: 45.6 us; the launch traced here: 45.5 us
  Pallas kernels  44.6 us (98%)
  between operations  0.8 us (2%)
    pallas_call x1, Pallas kernels, shards(): pl.pallas_call(functools.partial(kernel, groups, tiles, parts), out_shape...  41.9 us
    pallas_call x1, Pallas kernels, shards(): pl.pallas_call(functools.partial(write_out, 8), out_shape=(jax.ShapeDtype...  2.78 us

profile of v6, /device:TPU:1, one launch (start us, length us, event | category | flops | bytes accessed | tf_op | source)
XLA Modules:
  0.0 45.5 jit_solution(17200101242946219715)
XLA Ops:
  0.6 41.9 %shard_map.86 = (bf16[384,16,512]{2,1,0:T(8,128)(2,1)S(1)}, bf16[384,128]{1,0:T(8,128)(2,1)S(1)}) custom-call(s32[1,1,4]{2,1,0:T(1,128)} %picks.1, bf16[1,384,16,512]{3,2,1,0:T(8,128)(2,1)} %nest.1, bf16[384,128]{1,0:T(8,128)(2,1)} %parent.1, bf16[384,384]{1,0:T(8,128)(2,1)} %mix.1, bf16[1,1,4,128,512]{4,3,2,1,0:T(8,128)(2,1)} %interp.1, ...), custom_call_target="tpu_custom_call" | custom-call | tf_op jit(solution)/shard_map/pallas_call | solution.py:715
  42.5 2.8 %shard_map.87 = (bf16[1,384,16,512]{3,2,1,0:T(8,128)(2,1)}, bf16[384,128]{1,0:T(8,128)(2,1)}) custom-call(bf16[384,16,512]{2,1,0:T(8,128)(2,1)S(1)} %get-tuple-element.4.x, bf16[384,128]{1,0:T(8,128)(2,1)S(1)} %get-tuple-element.5.p), custom_call_target="tpu_custom_call" | custom-call | tf_op jit(solution)/shard_map/pallas_call | solution.py:762

commit v7 on v6

--- a/solution.py
+++ b/solution.py
@@ -20,14 +20,15 @@
 
 
 def kernel(
-    groups, tiles, parts,
+    groups, tiles, sizes,
     picks, nest, parent, mix, interp, avg, land,
     x_out, p_out,
     xa, xb, xf, ws, cand, hub_v, m_v, w_v, av_v, land_v, coef, strip_v, place_v, pack_v, ring_v, pool_v, tops, fb, fbs, r1, s2, r2, s3, r3, g1,
     load_sem, p_send, p_recv, d_send, d_recv, h_send, h_recv, s_send, s_recv, f_send, f_recv,
 ):
     channels, rows, width = x_out.shape
-    part = channels // parts
+    parts = len(sizes)
+    starts = [sum(sizes[:c]) for c in range(parts)]
     slots = w_v.shape[0]
     bands = rows // 4
     n, t = lax.axis_index("nest"), lax.axis_index("tile")
@@ -63,7 +64,10 @@
     pl.when(t == tiles // 2)(lambda: greet((deep, down)))
 
     def span(c):
-        return pl.ds(c * part, part)
+        return pl.ds(starts[c], sizes[c])
+
+    def held(c):
+        return pl.ds(0, sizes[c])
 
     x_loads = [pltpu.make_async_copy(nest.at[0, span(c)], x_out.at[span(c)], load_sem.at[c]) for c in range(parts)]
     own_load = pltpu.make_async_copy(parent, cand.at[3 * n + 1], load_sem.at[parts])
@@ -83,11 +87,11 @@
         x_loads[c].wait()
 
         def body(i, carry):
-            at = pl.ds(pl.multiple_of(c * part + i * 16, 16), 16)
+            at = pl.ds(pl.multiple_of(starts[c] + i * 16, 16), 16)
             xa[1 : rows + 1, at, :] = jnp.swapaxes(x_out[at], 0, 1)
             return carry
 
-        lax.fori_loop(0, part // 16, body, 0)
+        lax.fori_loop(0, sizes[c] // 16, body, 0)
 
     @pl.when(first)
     def _():
@@ -229,6 +233,7 @@
 
     land_load.wait()
     mix_load.wait()
+    m_v[...] = (1.25 * m_v[...].astype(f32)).astype(bf16)
     column = lax.broadcasted_iota(jnp.int32, (rows, width), 1)
     edge = jnp.minimum(column, width - 1 - column)
     ramp = jnp.maximum(BW - edge, 0).astype(f32) / BW
@@ -238,7 +243,7 @@
 
     def new_value(x, above, below, sides, mixed, mine, around):
         near = above + below + jnp.asarray(0.125, bf16) * sides
-        return mine * x.astype(f32) + around * (near.astype(f32) + 1.25 * mixed)
+        return mine * x.astype(f32) + around * (near.astype(f32) + mixed)
 
     def update(r, start, count):
         mixed = jnp.dot(m_v[start : start + count, :], xa[r + 1], preferred_element_type=f32)
@@ -261,17 +266,21 @@
     beside_row = jnp.logical_or(row_start, row_end)
     strip_early = jnp.logical_or(first, far)
     with jax.named_scope("first_inner"):
-        first_rows(0, 3)
+        first_rows(0, 1)
+    with jax.named_scope("tile_on"):
+
+        @pl.when(last)
+        def _():
+            from_below()
+            to_hub[1].start()
+            over_up.start()
+
+    with jax.named_scope("first_inner"):
+        first_rows(1, 3)
     with jax.named_scope("tile_on"):
         pl.when(after_first)(from_below)
         pl.when(jnp.logical_not(row_end))(from_above)
-        pl.when(jnp.logical_not(jnp.logical_or(row_start, after_first)))(from_below)
-
-
-        @pl.when(last)
-        def _():
-            to_hub[1].start()
-            over_up.start()
+        pl.when(jnp.logical_not(jnp.logical_or(row_start, jnp.logical_or(after_first, last))))(from_below)
 
         @pl.when(after_first)
         def _():
@@ -343,8 +352,14 @@
         with jax.named_scope("first_halo_wait"):
             halo_arrived(xa, 0, c)
         with jax.named_scope("first_edges"):
-            update(0, c * part, part)
-            update(rows - 1, c * part, part)
+            update(0, starts[c], sizes[c])
+            update(rows - 1, starts[c], sizes[c])
+
+    @pl.when(first)
+    def _():
+        pl.semaphore_wait(barrier, 2)
+        tile_down.start()
+        over_down.start()
 
     middle_quads(0, early)
     with jax.named_scope("tile_on"):
@@ -355,12 +370,6 @@
         def _():
             pl.semaphore_wait(barrier, 2)
             hub_pass(0)
-
-        @pl.when(first)
-        def _():
-            pl.semaphore_wait(barrier, 2)
-            tile_down.start()
-            over_down.start()
 
     middle_quads(early, sooner)
     first_edges(0)
@@ -385,7 +394,15 @@
     middle_quads(jnp.maximum(later, 2), 3)
     with jax.named_scope("tile_on"):
         pl.when(first)(from_below)
-        pl.when(last)(from_above)
+
+        @pl.when(last)
+        def _():
+            from_above()
+            over_down.wait_recv()
+            onward[2].start()
+            from_hub[0].wait_recv()
+            onward[1].start()
+
 
     cells = 2 * BW
     per = LANES // cells
@@ -411,12 +428,8 @@
 
             @pl.when(last)
             def _():
-                from_hub[0].wait_recv()
-                onward[1].start()
                 from_hub[1].wait_recv()
                 onward[0].start()
-                over_down.wait_recv()
-                onward[2].start()
 
         with jax.named_scope("core_tiles_wait"):
             for o in range(3):
@@ -456,7 +469,7 @@
         with jax.named_scope("strip_spread"):
             lax.fori_loop(0, per, spread, 0)
 
-    most = channels - part
+    most = starts[-1]
 
     def outer_quads(start, count):
         with jax.named_scope("second_outer"):
@@ -521,15 +534,17 @@
 
     up_group, down_group = jnp.where(over_above, deep, n), jnp.where(over_below, deep, n)
 
+    def core_copy(c, k, group):
+        i = 7 * c + k
+        blocks, landing = fbs.at[c, group, :, held(c)], r1.at[c, k, :, held(c)]
+        return remote(blocks, landing, f_send.at[i], f_recv.at[i], to_core)
+
     def core_copies(c):
-        return (
-            remote(fbs.at[c, core], r1.at[c, 0], f_send.at[7 * c], f_recv.at[7 * c], to_core),
-            remote(fbs.at[c, core_deep], r1.at[c, 1], f_send.at[7 * c + 1], f_recv.at[7 * c + 1], to_core),
-        )
+        return core_copy(c, 0, core), core_copy(c, 1, core_deep)
 
     def tile_copy(c, way, k, device):
         i = 7 * c + 2 + 2 * way + k
-        return remote(s2.at[c, way, k], r2.at[c, way, k], f_send.at[i], f_recv.at[i], device)
+        return remote(s2.at[c, way, k, held(c)], r2.at[c, way, k, held(c)], f_send.at[i], f_recv.at[i], device)
 
     def down_copies(c):
         return tile_copy(c, 0, 0, to_down), tile_copy(c, 0, 1, (down_group, down))
@@ -538,59 +553,63 @@
         return tile_copy(c, 1, 0, to_up), tile_copy(c, 1, 1, (up_group, up))
 
     def deep_copy(c):
-        return remote(s3.at[c], r3.at[c], f_send.at[7 * c + 6], f_recv.at[7 * c + 6], to_deep)
+        return remote(s3.at[c, held(c)], r3.at[c, held(c)], f_send.at[7 * c + 6], f_recv.at[7 * c + 6], to_deep)
 
     def stage_core(c):
         for copy in core_copies(c):
             copy.wait_recv()
         for k, group in enumerate((n, deep)):
-            total = fbs[c, group].astype(f32) + r1[c, k].astype(f32)
-            s2[c, 0, k] = total[0].astype(bf16)
-            s2[c, 1, k] = total[2].astype(bf16)
-            g1[c, k] = total[1]
+            total = fbs[c, group, :, held(c)].astype(f32) + r1[c, k, :, held(c)].astype(f32)
+            s2[c, 0, k, held(c)] = total[0].astype(bf16)
+            s2[c, 1, k, held(c)] = total[2].astype(bf16)
+            g1[c, k, held(c)] = total[1]
         for copy in (*down_copies(c), *up_copies(c)):
             copy.start()
 
     def stage_tile(c):
+        at = held(c)
+
         @pl.when(jnp.logical_not(over_above))
         def _():
             for copy in down_copies(c):
                 copy.wait_recv()
-            g1[c] = g1[c] + r2[c, 0].astype(f32)
+            g1[c, :, at] = g1[c, :, at] + r2[c, 0, :, at].astype(f32)
 
         @pl.when(jnp.logical_not(over_below))
         def _():
             for copy in up_copies(c):
                 copy.wait_recv()
-            g1[c] = g1[c] + r2[c, 1].astype(f32)
-
-        s3[c] = g1[c, 1].astype(bf16)
+            g1[c, :, at] = g1[c, :, at] + r2[c, 1, :, at].astype(f32)
+
+        s3[c, at] = g1[c, 1, at].astype(bf16)
         deep_copy(c).start()
 
     def stage_deep(c):
+        at = held(c)
+
         @pl.when(over_above)
         def _():
             for copy in down_copies(c):
                 copy.wait_recv()
-            g1[c, 0] = g1[c, 0] + r2[c, 0, 0].astype(f32) + r2[c, 0, 1].astype(f32)
+            g1[c, 0, at] = g1[c, 0, at] + r2[c, 0, 0, at].astype(f32) + r2[c, 0, 1, at].astype(f32)
 
         @pl.when(over_below)
         def _():
             for copy in up_copies(c):
                 copy.wait_recv()
-            g1[c, 0] = g1[c, 0] + r2[c, 1, 0].astype(f32) + r2[c, 1, 1].astype(f32)
+            g1[c, 0, at] = g1[c, 0, at] + r2[c, 1, 0, at].astype(f32) + r2[c, 1, 1, at].astype(f32)
 
         deep_copy(c).wait_recv()
         mine = cand[3 * n + 1, span(c), :].astype(f32)
-        p_out[span(c), :] = (mine + (g1[c, 0] + r3[c].astype(f32))).astype(bf16)
+        p_out[span(c), :] = (mine + (g1[c, 0, at] + r3[c, at].astype(f32))).astype(bf16)
 
     def channels_first(c):
         def body(i, carry):
-            at = pl.ds(pl.multiple_of(c * part + i * 16, 16), 16)
+            at = pl.ds(pl.multiple_of(starts[c] + i * 16, 16), 16)
             x_out[at] = jnp.swapaxes(xa[1 : rows + 1, at, :], 0, 1)
             return carry
 
-        lax.fori_loop(0, part // 16, body, 0)
+        lax.fori_loop(0, sizes[c] // 16, body, 0)
 
     feedback_inner(0, most)
 
@@ -601,29 +620,34 @@
     def halo_strip(c):
         for side, row in ((0, 0), (1, rows + 1)):
             for q in range(per):
-                begin, end = max(q * short, c * part), min((q + 1) * short, (c + 1) * part)
+                begin, end = max(q * short, starts[c]), min((q + 1) * short, starts[c] + sizes[c])
                 if begin < end:
                     at = slice(begin, end)
                     fixed(row, at, placed(ring_v[side, begin - q * short : end - q * short, :], q))
 
     for c in range(parts):
         halo_sent(xa, 0, c)
+    def last_part():
+        outer_quads(starts[-1], sizes[-1])
+        outer_near(starts[-1], sizes[-1])
+        feedback_inner(starts[-1], sizes[-1])
+
     for c in range(parts):
+        if c == 1:
+            pl.when(far)(last_part)
         if c == parts - 1:
-            outer_quads(c * part, part)
-            outer_near(c * part, part)
-            feedback_inner(c * part, part)
+            pl.when(jnp.logical_not(far))(last_part)
             with jax.named_scope("feedback_core"):
-                for k in range(c):
-                    stage_core(k)
+                stage_core(0)
+                pl.when(jnp.logical_not(far))(lambda: stage_core(1))
         with jax.named_scope("second_halo_wait"):
             halo_arrived(xb, 1, c)
         with jax.named_scope("second_edges"):
             halo_strip(c)
             for r in (0, rows - 1):
-                update_mid(r, c * part, part)
-                update_out(r, c * part, part)
-        at = slice(c * part, (c + 1) * part)
+                update_mid(r, starts[c], sizes[c])
+                update_out(r, starts[c], sizes[c])
+        at = slice(starts[c], starts[c] + sizes[c])
         with jax.named_scope("feedback_edges"):
             low_band = averaged(tops[0, at, :] + xa[1, at, :].astype(f32))
             high_band = averaged(tops[1, at, :] + xa[rows, at, :].astype(f32))
@@ -631,12 +655,14 @@
             terms = terms + jnp.dot(high_band, av_v[(bands - 1) * LANES :, :], preferred_element_type=f32)
         with jax.named_scope("feedback_slots"):
             for slot in range(3 * groups):
-                total = jnp.zeros((part, LANES), f32)
+                total = jnp.zeros((sizes[c], LANES), f32)
                 for k in range(slots):
                     total = total + (picks[0, 0, k] == slot).astype(f32) * terms[:, k * LANES : (k + 1) * LANES]
-                fbs[c, slot // 3, slot % 3] = total.astype(bf16)
+                fbs[c, slot // 3, slot % 3, held(c)] = total.astype(bf16)
             for copy in core_copies(c):
                 copy.start()
+    with jax.named_scope("feedback_core"):
+        pl.when(far)(lambda: stage_core(1))
     with jax.named_scope("channels_first"):
         channels_first(0)
     with jax.named_scope("feedback_core"):
@@ -708,12 +734,12 @@
     groups, tiles = lax.axis_size("nest"), lax.axis_size("tile")
     slots = intersection.shape[2]
     cells = parent_state.shape[1]
-    parts = 3
-    part = channels // parts
+    sizes = (channels // 3,) * 3
+    parts, part = len(sizes), max(sizes)
     hbm = pl.BlockSpec(memory_space=pl.ANY)
     vmem = pl.BlockSpec(memory_space=pltpu.VMEM)
     x_new, p_new = pl.pallas_call(
-        functools.partial(kernel, groups, tiles, parts),
+        functools.partial(kernel, groups, tiles, sizes),
         out_shape=(pltpu.VMEM((channels, rows, width), bf16), pltpu.VMEM((channels, cells), bf16)),
         in_specs=[pl.BlockSpec(memory_space=pltpu.SMEM)] + [hbm] * 6,
         out_specs=(vmem, vmem),

time: 45.6 us -> 46 us (level)
  Pallas kernels: 44.6 us -> 45.1 us
where the time goes in v7:
time: 46 us; the launch traced here: 45.9 us
  Pallas kernels  45.1 us (98%)
  between operations  0.8 us (2%)
    pallas_call x1, Pallas kernels, shards(): pl.pallas_call(functools.partial(kernel, groups, tiles, sizes), out_shape...  42.3 us
    pallas_call x1, Pallas kernels, shards(): pl.pallas_call(functools.partial(write_out, 8), out_shape=(jax.ShapeDtype...  2.78 us

profile of v7, /device:TPU:1, one launch (start us, length us, event | category | flops | bytes accessed | tf_op | source)
XLA Modules:
  0.0 45.9 jit_solution(4812560440353361019)
XLA Ops:
  0.6 42.3 %shard_map.86 = (bf16[384,16,512]{2,1,0:T(8,128)(2,1)S(1)}, bf16[384,128]{1,0:T(8,128)(2,1)S(1)}) custom-call(s32[1,1,4]{2,1,0:T(1,128)} %picks.1, bf16[1,384,16,512]{3,2,1,0:T(8,128)(2,1)} %nest.1, bf16[384,128]{1,0:T(8,128)(2,1)} %parent.1, bf16[384,384]{1,0:T(8,128)(2,1)} %mix.1, bf16[1,1,4,128,512]{4,3,2,1,0:T(8,128)(2,1)} %interp.1, ...), custom_call_target="tpu_custom_call" | custom-call | tf_op jit(solution)/shard_map/pallas_call | solution.py:741
  43.0 2.8 %shard_map.87 = (bf16[1,384,16,512]{3,2,1,0:T(8,128)(2,1)}, bf16[384,128]{1,0:T(8,128)(2,1)}) custom-call(bf16[384,16,512]{2,1,0:T(8,128)(2,1)S(1)} %get-tuple-element.4.x, bf16[384,128]{1,0:T(8,128)(2,1)S(1)} %get-tuple-element.5.p), custom_call_target="tpu_custom_call" | custom-call | tf_op jit(solution)/shard_map/pallas_call | solution.py:788
